TPU v7x, 256 devices: a whole 4x4x8 slice. The times are simulated.
256 devices in a mesh: anc: 32 (over x, y, core), cand: 8 (over z).
Axes of the slice: x: 4, y: 4, z: 8, core: 2. Of those that a mesh axis runs over, the one named last changes fastest.
Arguments:
- anchors: float32 [32768, 256], P('anc'), may hold values from -300 to 300
- candidates: float32 [32768, 256], P('cand'), may hold values from -20 to 20
- positives: int32 [32768], P('anc'), may hold values from 0 to 32767
Outputs:
- mean_loss: float32 [], replicated
- anchor_grad: float32 [32768, 256], P(('anc', 'cand'))
- cand_grad: float32 [8, 4096, 256], P('cand', 'anc')
All inputs are finite; a program needn't handle non-finite values.
Results may differ from a plain program's by a relative error of at most 0.0003.
Values sent between devices are 32-bit elements; how exact they have to be, the bound alone decides.
A program may use at most 128 MiB of HBM per device.

v0:
```python
import math

import jax
import jax.numpy as jnp
from jax import lax
from jax.sharding import PartitionSpec as P


def product(left, right):
    return jnp.dot(left, right, precision=lax.Precision.HIGHEST, preferred_element_type=jnp.float32)


def body(anchors, candidates, positives):
    rows = anchors.shape[0]
    width = anchors.shape[1]
    cand_rows = candidates.shape[0]
    scale = 0.25 / math.sqrt(width)
    offset = lax.axis_index("cand") * cand_rows
    logits = product(anchors, candidates.T) * scale
    columns = offset + lax.broadcasted_iota(jnp.int32, (1, cand_rows), 1)
    hit = columns == positives[:, None]
    local_positive = jnp.sum(jnp.where(hit, logits, jnp.zeros_like(logits)), axis=1)
    local_max = jnp.max(logits, axis=1)
    row_max = lax.pmax(local_max, "cand")
    local_total = jnp.sum(jnp.exp(logits - row_max[:, None]), axis=1)
    total, positive_logit = lax.psum((local_total, local_positive), "cand")
    lse = row_max + jnp.log(total)
    loss_total = lax.psum(jnp.sum(lse - positive_logit), "anc")
    mean_loss = loss_total / (rows * lax.axis_size("anc"))
    weights = jnp.exp(logits - lse[:, None]) - hit.astype(jnp.float32)
    anchor_grad = lax.psum_scatter(
        product(weights, candidates) * scale, "cand", scatter_dimension=0, tiled=True
    )
    cand_grad = lax.psum_scatter(
        product(weights.T, anchors) * scale, "anc", scatter_dimension=0, tiled=True
    )
    return (mean_loss, anchor_grad, cand_grad[None])


def solution(mesh):
    in_specs = (P("anc", None), P("cand", None), P("anc"))
    out_specs = (P(), P(("anc", "cand"), None), P("cand", "anc", None))
    return jax.shard_map(body, mesh=mesh, in_specs=in_specs, out_specs=out_specs, check_vma=False)
```

profile of v0, /device:TPU:1, one launch (start us, length us, event | category | flops | bytes accessed | tf_op | source)
XLA Modules:
  0.0 230.5 jit_solution(1032150679537242519)
XLA Ops:
  7.2 0.0 copy-start
  7.2 0.0 copy-start.1
  7.2 0.0 reduce-scatter.3.cloned.1.call-start
  7.3 1.1 copy-done
  8.4 17.8 %multiply_reduce_fusion = (f32[1024]{0:T(1024)S(1)}, f32[1024,4096]{1,0:T(8,128)}) fusion(f32[1024,256]{1,0:T(8,128)S(1)} %copy-done, f32[4096,256]{1,0:T(8,128)} %param.4), kind=kOutput, calls=%fused_computation.5 | convolution fusion | flops 12893289472 | bytes 22024192 | tf_op jit(solution)/shard_map/dot_general | solution.py:10
  26.2 17.3 %pmax.7 = f32[1024]{0:T(1024)S(1)} all-reduce(f32[1024]{0:T(1024)S(1)} %get-tuple-element.9), channel_id=1, replica_groups=mesh['anc'=32,'cand'=8] {'cand'}, use_global_device_ids=true, to_apply=%region_1.2 | all-reduce | flops 1024 | bytes 8192 | tf_op jit(solution)/shard_map/pmax | solution.py:24
  43.4 0.0 copy-done.1
  43.4 8.8 %fusion = (f32[1024]{0:T(1024)S(1)}, f32[1024]{0:T(1024)S(1)}) fusion(f32[1024,4096]{1,0:T(8,128)} %get-tuple-element.10, s32[4096]{0:T(1024)S(1)} %iota_add_fusion, s32[1024]{0:T(1024)S(1)} %copy-done.1, f32[1024]{0:T(1024)S(1)} %pmax.7), kind=kLoop, calls=%fused_computation.2 | loop fusion | flops 25163776 | bytes 16809984 | tf_op jit(solution)/shard_map/reduce_sum | solution.py:22
  52.3 11.1 %all-reduce = (f32[1024]{0:T(1024)S(1)}, f32[1024]{0:T(1024)S(1)}) all-reduce(f32[1024]{0:T(1024)S(1)} %get-tuple-element.4, f32[1024]{0:T(1024)S(1)} %get-tuple-element.3), channel_id=1, replica_groups=mesh['anc'=32,'cand'=8] {'cand'}, use_global_device_ids=true, to_apply=%region_3.4 | all-reduce | flops 2048 | bytes 16384 | tf_op jit(solution)/shard_map/psum | solution.py:26
  63.4 0.6 subtract_reduce_fusion
  64.0 22.4 %fusion.17 = f32[1024,256]{1,0:T(8,128)} fusion(f32[4096,256]{1,0:T(8,128)} %param.4, f32[1024,4096]{1,0:T(8,128)} %get-tuple-element.10, f32[1024]{0:T(1024)S(1)} %get-tuple-element.8, s32[4096]{0:T(1024)S(1)} %iota_add_fusion, s32[1024]{0:T(1024)S(1)} %copy-done.1), kind=kOutput, calls=%fused_computation.17 | convolution fusion | flops 12906135552 | bytes 22044672 | tf_op jit(solution)/shard_map/dot_general | solution.py:10
  86.4 0.0 reduce-scatter.3.cloned.1.call-update
  86.4 0.3 reduce-scatter.5.cloned.1.call-start
  86.7 32.6 %fusion.14 = f32[4096,256]{1,0:T(8,128)} fusion(f32[1024,256]{1,0:T(8,128)S(1)} %copy-done, f32[1024,4096]{1,0:T(8,128)} %get-tuple-element.10, f32[1024]{0:T(1024)S(1)} %get-tuple-element.8, s32[4096]{0:T(1024)S(1)} %iota_add_fusion, s32[1024]{0:T(1024)S(1)} %copy-done.1), kind=kOutput, calls=%fused_computation.16 | convolution fusion | flops 12906921984 | bytes 22044672 | tf_op jit(solution)/shard_map/dot_general | solution.py:10
  119.3 0.0 reduce-scatter.5.cloned.1.call-update
  119.3 70.6 %psum.23 = f32[]{:T(128)} all-reduce(f32[]{:T(128)} %get-tuple-element.7), channel_id=1, replica_groups=mesh['anc'=32,'cand'=8] {'anc'}, use_global_device_ids=true, to_apply=%region_7.8 | all-reduce | flops 1 | bytes 8 | tf_op jit(solution)/shard_map/psum | solution.py:28
  190.6 0.0 reduce-scatter.3.cloned.1.call-done
  190.6 31.9 %reduce-scatter.5.cloned.1.call-done = f32[128,256]{1,0:T(8,128)} async-done(((f32[4096,256]{1,0:T(8,128)}), f32[128,256]{1,0:T(8,128)}) %reduce-scatter.5.cloned.1.call-update) | async-done | bytes 131088 | tf_op jit(solution)/shard_map/reduce_scatter | solution.py:34
  (1 shorter events, 0.0 us)
Async XLA Ops:
  7.2 1.2 copy-start
  7.2 36.3 %copy-start.1 = (s32[1024]{0:T(1024)S(1)}, s32[1024]{0:T(1024)}, u32[]{:S(2)}) copy-start(s32[1024]{0:T(1024)} %param.5) | copy-start | bytes 12292
  7.2 183.4 %reduce-scatter.3.cloned.1.call-start = ((), (), s32[]{:S(2)}) async-start(), calls=%async_computation.2 | async-start | bytes 1179648 | tf_op jit(solution)/shard_map/reduce_scatter | solution.py:31
  86.4 136.1 %reduce-scatter.5.cloned.1.call-start = ((), (), s32[]{:S(2)}) async-start(), calls=%async_computation.3 | async-start | bytes 4325376 | tf_op jit(solution)/shard_map/reduce_scatter | solution.py:34
Sparse Core Ops, SparseCore 0:
  86.5 40.2 reduce-scatter.2
  131.3 91.0 reduce-scatter.4
where the time goes:
time: 231 us; the launch traced here: 230 us
  blocking collectives  99 us (43%)
  matrix products  72.7 us (31%)
  waiting for transfers between devices  31.9 us (14%)
  between operations  15.9 us (7%)
  other arithmetic  9.43 us (4%)
    dot_general x3, matrix products, product(): jnp.dot(left, right, precision=lax.Precision.HIGHEST, preferred_element_t...  72.7 us
    psum x1, blocking collectives, body(): loss_total = lax.psum(jnp.sum(lse - positive_logit), 'anc')  70.6 us
    reduce_scatter x1, waiting for transfers between devices, body(): lax.psum_scatter(product(weights.T, anchors) * scale, 'anc', scatter_dime...  31.9 us
    pmax x1, blocking collectives, body(): row_max = lax.pmax(local_max, 'cand')  17.3 us
    psum x1, blocking collectives, body(): total, positive_logit = lax.psum((local_total, local_positive), 'cand')  11.1 us
    reduce_sum x1, other arithmetic, body(): jnp.sum(jnp.where(hit, logits, jnp.zeros_like(logits)), axis=1)  8.82 us
  transfers between devices with their start and end apart: 2, of which 1 were waited for; matrix products, arithmetic and copies ran while one was open for 14% of the time, Pallas kernels for 0%

commit v1 on v0

v1 whole, which is shorter than its diff:
```python
import math

import jax
import jax.numpy as jnp
from jax import lax
from jax.experimental import pallas as pl
from jax.experimental.pallas import tpu as pltpu
from jax.sharding import PartitionSpec as P

F32 = jnp.float32
BF16 = jnp.bfloat16
WIDTH = 256
ANCHORS = 1024
CANDS = 4096
TILE = 512
TILES = CANDS // TILE
LOG2E = math.log2(math.e)
LN2 = math.log(2.0)
SCALE = 0.25 / math.sqrt(WIDTH)
SLABS = (2, 1, 3, 0)
PAIRS = ((4, 3), (5, 2), (6, 1), (7, 0))


def split(value):
    high = value.astype(BF16)
    return high, (value - high.astype(F32)).astype(BF16)


def dot(left, right):
    return jnp.dot(left, right, preferred_element_type=F32)


def dot_nt(left, right):
    return lax.dot_general(left, right, (((1,), (1,)), ((), ())), preferred_element_type=F32)


class Copies:
    def __init__(self, send_sems, recv_sems):
        self.send_sems, self.recv_sems = send_sems, recv_sems
        self.made = []

    def start(self, source, target, device):
        index = len(self.made)
        copy = pltpu.make_async_remote_copy(
            src_ref=source,
            dst_ref=target,
            send_sem=self.send_sems.at[index],
            recv_sem=self.recv_sems.at[index],
            device_id=device,
            device_id_type=pl.DeviceIdType.MESH,
        )
        copy.start()
        self.made.append(copy)
        return copy


def kernel(
    a_ref, c_ref, pos_ref, loss_ref, agrad_ref, cgrad_ref,
    c_hi, c_lo, ct_hi, ct_lo, al_hi, al_lo, as_hi, as_lo,
    p_ref, w_hi, w_lo, stat, back, stat_rx, loss_rx,
    slab, pair_rx, q0, q1, x0, y1, rx0, rx1, ry0, ry1, grad, z_rx,
    send_sems, recv_sems,
):
    anc = lax.axis_index("anc")
    z = lax.axis_index("cand")
    x, y, core = anc // 8, lax.rem(anc // 2, 4), lax.rem(anc, 2)

    def at(dx=0, dy=0, other=False, dz=0):
        px = lax.rem(x + dx, 4)
        py = lax.rem(y + dy, 4)
        pc = 1 - core if other else core
        return ((px * 4 + py) * 2 + pc, lax.rem(z + dz, 8))

    peers = [at(other=True)]
    peers += [at(dx=d) for d in (1, 2, 3)] + [at(dy=d) for d in (1, 2, 3)]
    peers += [at(dz=d) for d in range(1, 8)]
    barrier = pltpu.get_barrier_semaphore()
    for peer in peers:
        pl.semaphore_signal(barrier, inc=1, device_id=peer, device_id_type=pl.DeviceIdType.MESH)

    copies = Copies(send_sems, recv_sems)
    rows_iota = lax.broadcasted_iota(jnp.int32, (TILE, 1), 0)

    al_hi[...], al_lo[...] = split(a_ref[...] * (SCALE * LOG2E))
    as_hi[...], as_lo[...] = split(a_ref[...] * SCALE)

    @pl.loop(0, TILES)
    def _(j):
        rows = pl.ds(pl.multiple_of(j * TILE, TILE), TILE)
        block = c_ref[rows, :]
        ch, cl = split(block)
        c_hi[rows, :], c_lo[rows, :] = ch, cl
        th, tl = split((block * SCALE).T)
        ct_hi[j], ct_lo[j] = th, tl
        left = jnp.concatenate([ch, cl, ch], axis=1)
        first = z * CANDS + j * TILE
        for i in range(4):
            lanes = slice(i * 256, (i + 1) * 256)
            ah, al = al_hi[lanes, :], al_lo[lanes, :]
            logits = dot_nt(left, jnp.concatenate([ah, ah, al], axis=1))
            hit = rows_iota == pos_ref[0:1, lanes] - first
            top = jnp.max(logits, axis=0, keepdims=True)
            stat[j, 2:3, lanes] = jnp.sum(jnp.where(hit, logits, 0.0), axis=0, keepdims=True)
            prob = jnp.exp2(logits - top)
            stat[j, 0:1, lanes] = top
            stat[j, 1:2, lanes] = jnp.sum(prob, axis=0, keepdims=True)
            p_ref[rows, lanes] = prob

    tops = [stat[j, 0:1, :] for j in range(TILES)]
    top = tops[0]
    for j in range(1, TILES):
        top = jnp.maximum(top, tops[j])
    total = jnp.zeros_like(top)
    chosen = jnp.zeros_like(top)
    for j in range(TILES):
        total += stat[j, 1:2, :] * jnp.exp2(tops[j] - top)
        chosen += stat[j, 2:3, :]
    for k in range(8):
        lanes = slice(k * 128, (k + 1) * 128)
        stat_rx[z, 0, k:k + 1, :] = top[:, lanes]
        stat_rx[z, 1, k:k + 1, :] = total[:, lanes]
        stat_rx[z, 2, k:k + 1, :] = chosen[:, lanes]

    pl.semaphore_wait(barrier, len(peers))
    sent = [copies.start(stat_rx.at[z], stat_rx.at[z], at(dz=d)) for d in range(1, 8)]
    for copy in sent:
        copy.wait_recv()
    top = stat_rx[0, 0]
    for k in range(1, 8):
        top = jnp.maximum(top, stat_rx[k, 0])
    total = jnp.zeros_like(top)
    chosen = jnp.zeros_like(top)
    for k in range(8):
        total += stat_rx[k, 1] * jnp.exp2(stat_rx[k, 0] - top)
        chosen += stat_rx[k, 2]
    lse = top + jnp.log2(total)
    loss_rx[0, core] = (lse - chosen) * LN2
    loss_copy = copies.start(loss_rx.at[0, core], loss_rx.at[0, core], at(other=True))
    lse_row = jnp.concatenate([lse[k:k + 1, :] for k in range(8)], axis=1)
    for j in range(TILES):
        back[j] = jnp.exp2(stat[j, 0:1, :] - lse_row)

    def cand_slab(s):
        px = lax.rem(x + SLABS[s], 4)

        @pl.loop(0, 2)
        def _(half):
            j = px * 2 + half
            rows = pl.ds(pl.multiple_of(j * TILE, TILE), TILE)
            first = z * CANDS + j * TILE
            highs, lows = [], []
            for k in range(8):
                lanes = slice(k * 128, (k + 1) * 128)
                weight = p_ref[rows, lanes] * back[j, :, lanes]
                hit = rows_iota == pos_ref[0:1, lanes] - first
                wh, wl = split(jnp.where(hit, weight - 1.0, weight))
                w_hi[k, rows, :], w_lo[k, rows, :] = wh, wl
                highs.append(wh)
                lows.append(wl)
            wh, wl = jnp.concatenate(highs, axis=1), jnp.concatenate(lows, axis=1)
            part = dot(wh, as_hi[...]) + dot(wl, as_hi[...]) + dot(wh, as_lo[...])
            for q in range(4):
                slab[s, half * 2 + q // 2, q % 2] = part[q * 128:(q + 1) * 128, :]

        return copies.start(slab.at[s, :, 1 - core], pair_rx.at[s], at(other=True))

    def pair_sum(s, copy):
        copy.wait_recv()
        for dy in range(4):
            py = lax.rem(y + dy, 4)
            both = slab[s, py, core] + pair_rx[s, py]
            q0[s, dy] = both[:, :128]
            q1[dy, s] = both[:, 128:]

    def anchor_pair(pair):
        places = [lax.rem(z + d, 8) for d in pair]
        acc = None
        for j in range(TILES):
            rows = slice(j * TILE, (j + 1) * TILE)
            wh = jnp.concatenate([w_hi[p, rows, :] for p in places], axis=1)
            wl = jnp.concatenate([w_lo[p, rows, :] for p in places], axis=1)
            part = dot(ct_hi[j], wh) + dot(ct_lo[j], wh) + dot(ct_hi[j], wl)
            acc = part if acc is None else acc + part
        for n, d in enumerate(pair):
            for h in range(2):
                grad[d, h] = acc[h * 128:(h + 1) * 128, n * 128:(n + 1) * 128]

    z_right, z_left = {}, {}

    def send_right(d, h):
        slot = len(z_right) + len(z_left)
        z_right[d - 1, h] = (slot, copies.start(grad.at[d, h], z_rx.at[slot], at(dz=1)))

    def send_left(d, h):
        slot = len(z_right) + len(z_left)
        z_left[(d + 1) % 8, h] = (slot, copies.start(grad.at[d, h], z_rx.at[slot], at(dz=7)))

    def add_to(side, d, h):
        slot, copy = side[d, h]
        copy.wait_recv()
        grad[d, h] = grad[d, h] + z_rx[slot]

    def pass_right(d, h):
        add_to(z_right, d, h)
        send_right(d, h)

    def pass_left(d, h):
        add_to(z_left, d, h)
        send_left(d, h)

    right_x, left_x, right_y, left_y = at(dx=1), at(dx=3), at(dy=1), at(dy=3)

    pair0 = cand_slab(0)
    loss_copy.wait_recv()
    loss_rx[1, x] = loss_rx[0, 0] + loss_rx[0, 1]
    loss_copies = [copies.start(loss_rx.at[1, x], loss_rx.at[1, x], at(dx=d)) for d in (1, 2, 3)]

    pair1 = cand_slab(1)
    pair_sum(0, pair0)
    x_far_r = copies.start(q0.at[0, 0:2], rx0.at[0], right_x)
    x_far_l = copies.start(q0.at[0, 2:4], rx0.at[1], left_x)
    for copy in loss_copies:
        copy.wait_recv()
    loss_rx[2, y] = (loss_rx[1, 0] + loss_rx[1, 1]) + (loss_rx[1, 2] + loss_rx[1, 3])
    loss_copies = [copies.start(loss_rx.at[2, y], loss_rx.at[2, y], at(dy=d)) for d in (1, 2, 3)]

    pair2 = cand_slab(2)
    pair_sum(1, pair1)
    x_near = [copies.start(q0.at[1, 2:4], rx0.at[2], right_x)]
    y_far_r = copies.start(q1.at[2, 0:2], ry1.at[0], right_y)
    y_near = [copies.start(q1.at[3, 0:2], ry1.at[1], left_y)]
    x_far_r.wait_recv()
    q0[1, 0:2] = q0[1, 0:2] + rx0[0]
    x_near.append(copies.start(q0.at[1, 0:2], rx0.at[3], right_x))

    pair3 = cand_slab(3)
    pair_sum(2, pair2)
    x_near.append(copies.start(q0.at[2, 0:2], rx0.at[4], left_x))
    x_far_l.wait_recv()
    q0[2, 2:4] = q0[2, 2:4] + rx0[1]
    x_near.append(copies.start(q0.at[2, 2:4], rx0.at[5], left_x))
    y_far_r.wait_recv()
    q1[1, 0:2] = q1[1, 0:2] + ry1[0]
    y_near.append(copies.start(q1.at[1, 0:2], ry1.at[2], right_y))
    for copy in loss_copies:
        copy.wait_recv()
    losses = (loss_rx[2, 0] + loss_rx[2, 1]) + (loss_rx[2, 2] + loss_rx[2, 3])
    loss_ref[...] = jnp.sum(losses, keepdims=True) * (1.0 / (32 * ANCHORS))

    anchor_pair(PAIRS[0])
    send_right(4, 0)
    send_left(4, 1)
    send_right(3, 1)
    pair_sum(3, pair3)
    y_far_l = copies.start(q1.at[2, 2:4], ry1.at[3], left_y)
    y_near.append(copies.start(q1.at[1, 2:4], ry1.at[4], right_y))
    for copy in x_near:
        copy.wait_recv()
    x0[0:2] = q0[3, 0:2] + rx0[3] + rx0[4]
    x0[2:4] = q0[3, 2:4] + rx0[2] + rx0[5]
    f_far_r = copies.start(x0.at[2, 0:64], ry0.at[0], right_y)
    f_far_l = copies.start(x0.at[2, 64:128], ry0.at[1], left_y)
    f_near = [
        copies.start(x0.at[1, 64:128], ry0.at[2], right_y),
        copies.start(x0.at[3, 0:64], ry0.at[3], left_y),
    ]

    anchor_pair(PAIRS[1])
    send_left(5, 0)
    pass_right(3, 0)
    pass_right(2, 1)
    pass_left(5, 1)
    y_far_l.wait_recv()
    q1[3, 2:4] = q1[3, 2:4] + ry1[3]
    y_near.append(copies.start(q1.at[3, 2:4], ry1.at[5], left_y))
    f_far_r.wait_recv()
    x0[1, 0:64] = x0[1, 0:64] + ry0[0]
    f_near.append(copies.start(x0.at[1, 0:64], ry0.at[4], right_y))
    f_far_l.wait_recv()
    x0[3, 64:128] = x0[3, 64:128] + ry0[1]
    f_near.append(copies.start(x0.at[3, 64:128], ry0.at[5], left_y))

    anchor_pair(PAIRS[2])
    pass_right(2, 0)
    pass_right(1, 1)
    pass_left(6, 0)
    pass_left(6, 1)
    for copy in y_near:
        copy.wait_recv()
    y1[0:2] = q1[0, 0:2] + ry1[1] + ry1[2]
    y1[2:4] = q1[0, 2:4] + ry1[4] + ry1[5]
    s_far_r = copies.start(y1.at[0, 0:64], rx1.at[0], right_x)
    s_far_l = copies.start(y1.at[0, 64:128], rx1.at[1], left_x)
    s_near = [
        copies.start(y1.at[1, 64:128], rx1.at[2], right_x),
        copies.start(y1.at[2, 0:64], rx1.at[3], left_x),
    ]
    for copy in f_near:
        copy.wait_recv()
    cgrad_ref[0:64, 0:128] = x0[0, 0:64] + ry0[4] + ry0[3]
    cgrad_ref[64:128, 0:128] = x0[0, 64:128] + ry0[2] + ry0[5]

    anchor_pair(PAIRS[3])
    pass_right(1, 0)
    pass_left(7, 0)
    pass_left(7, 1)
    s_far_r.wait_recv()
    y1[1, 0:64] = y1[1, 0:64] + rx1[0]
    s_near.append(copies.start(y1.at[1, 0:64], rx1.at[4], right_x))
    s_far_l.wait_recv()
    y1[2, 64:128] = y1[2, 64:128] + rx1[1]
    s_near.append(copies.start(y1.at[2, 64:128], rx1.at[5], left_x))

    for h in range(2):
        add_to(z_right, 0, h)
        add_to(z_left, 0, h)
        agrad_ref[:, h * 128:(h + 1) * 128] = grad[0, h].T
    for copy in s_near:
        copy.wait_recv()
    cgrad_ref[0:64, 128:256] = y1[3, 0:64] + rx1[4] + rx1[3]
    cgrad_ref[64:128, 128:256] = y1[3, 64:128] + rx1[2] + rx1[5]
    for copy in copies.made:
        copy.wait_send()


def body(anchors, candidates, positives):
    vmem = pl.BlockSpec(memory_space=pltpu.VMEM)
    sems = 64
    loss, anchor_grad, cand_grad = pl.pallas_call(
        kernel,
        out_shape=[
            jax.ShapeDtypeStruct((1, 1), F32),
            jax.ShapeDtypeStruct((128, WIDTH), F32),
            jax.ShapeDtypeStruct((128, WIDTH), F32),
        ],
        in_specs=[vmem] * 3,
        out_specs=[vmem] * 3,
        scratch_shapes=[
            pltpu.VMEM((CANDS, WIDTH), BF16),
            pltpu.VMEM((CANDS, WIDTH), BF16),
            pltpu.VMEM((TILES, WIDTH, TILE), BF16),
            pltpu.VMEM((TILES, WIDTH, TILE), BF16),
            pltpu.VMEM((ANCHORS, WIDTH), BF16),
            pltpu.VMEM((ANCHORS, WIDTH), BF16),
            pltpu.VMEM((ANCHORS, WIDTH), BF16),
            pltpu.VMEM((ANCHORS, WIDTH), BF16),
            pltpu.VMEM((CANDS, ANCHORS), F32),
            pltpu.VMEM((8, CANDS, 128), BF16),
            pltpu.VMEM((8, CANDS, 128), BF16),
            pltpu.VMEM((TILES, 8, ANCHORS), F32),
            pltpu.VMEM((TILES, 1, ANCHORS), F32),
            pltpu.VMEM((8, 3, 8, 128), F32),
            pltpu.VMEM((3, 4, 8, 128), F32),
            pltpu.VMEM((4, 4, 2, 128, WIDTH), F32),
            pltpu.VMEM((4, 4, 128, WIDTH), F32),
            pltpu.VMEM((4, 4, 128, 128), F32),
            pltpu.VMEM((4, 4, 128, 128), F32),
            pltpu.VMEM((4, 128, 128), F32),
            pltpu.VMEM((4, 128, 128), F32),
            pltpu.VMEM((6, 2, 128, 128), F32),
            pltpu.VMEM((6, 64, 128), F32),
            pltpu.VMEM((6, 64, 128), F32),
            pltpu.VMEM((6, 2, 128, 128), F32),
            pltpu.VMEM((8, 2, 128, 128), F32),
            pltpu.VMEM((14, 128, 128), F32),
            pltpu.SemaphoreType.DMA((sems,)),
            pltpu.SemaphoreType.DMA((sems,)),
        ],
        compiler_params=pltpu.CompilerParams(
            collective_id=0, has_side_effects=True, vmem_limit_bytes=63 << 20
        ),
    )(anchors, candidates, positives.reshape(1, ANCHORS))
    return (loss.reshape(()), anchor_grad, cand_grad[None])


def solution(mesh):
    in_specs = (P("anc", None), P("cand", None), P("anc"))
    out_specs = (P(), P(("anc", "cand"), None), P("cand", "anc", None))
    return jax.shard_map(body, mesh=mesh, in_specs=in_specs, out_specs=out_specs, check_vma=False)
```

time: 231 us -> 69.2 us (0.30)
  the two profiles are of different devices: /device:TPU:1 before, /device:TPU:16 now
where the time goes in v1:
time: 69.2 us; the launch traced here: 69.1 us
  Pallas kernels  63.5 us (92%)
  local copies, waits for them, and re-layouts  3.14 us (5%)
  between operations  2.4 us (3%)
    pallas_call x1, Pallas kernels, body(): pl.pallas_call(kernel, out_shape=[jax.ShapeDtypeStruct((1, 1), F32), jax....  63.5 us
    unnamed x2, local copies, waits for them, and re-layouts  3.14 us

profile of v1, /device:TPU:16, one launch (start us, length us, event | category | flops | bytes accessed | tf_op | source)
XLA Modules:
  0.0 69.1 jit_solution(9841328476221802203)
XLA Ops:
  0.6 63.5 %shard_map.58 = (f32[1,1]{1,0:T(1,128)}, f32[128,256]{1,0:T(8,128)}, f32[128,256]{1,0:T(8,128)}) custom-call(f32[1024,256]{1,0:T(8,128)} %a_ref.1, f32[4096,256]{1,0:T(8,128)} %c_ref.1, s32[1,1024]{1,0:T(1,128)} %bitcast.4), custom_call_target="tpu_custom_call" | custom-call | tf_op jit(solution)/shard_map/pallas_call | solution.py:329
  64.8 1.6 %copy.10 = f32[128,256]{1,0:T(8,128)} copy(f32[128,256]{1,0:T(8,128)} %get-tuple-element.13) | data formatting | bytes 262144
  66.4 1.6 %copy.11 = f32[1,128,256]{2,1,0:T(8,128)} copy(f32[1,128,256]{2,1,0:T(8,128)} %bitcast.3) | data formatting | bytes 262144

commit v2 on v0

v2 whole, which is shorter than its diff:
```python
import math

import jax
import jax.numpy as jnp
from jax import lax
from jax.experimental import pallas as pl
from jax.experimental.pallas import tpu as pltpu
from jax.sharding import PartitionSpec as P

F32 = jnp.float32
BF16 = jnp.bfloat16
WIDTH = 256
ANCHORS = 1024
CANDS = 4096
TILE = 512
TILES = CANDS // TILE
LOG2E = math.log2(math.e)
LN2 = math.log(2.0)
SCALE = 0.25 / math.sqrt(WIDTH)
BLOCK = 256
AWAY = (2, 1, 3)


def split(value):
    high = value.astype(BF16)
    return high, (value - high.astype(F32)).astype(BF16)


def dot(left, right):
    return jnp.dot(left, right, preferred_element_type=F32)


def dot_nt(left, right):
    return lax.dot_general(left, right, (((1,), (1,)), ((), ())), preferred_element_type=F32)


class Copies:
    def __init__(self, send_sems, recv_sems):
        self.send_sems, self.recv_sems = send_sems, recv_sems
        self.made = []

    def start(self, source, target, device):
        index = len(self.made)
        copy = pltpu.make_async_remote_copy(
            src_ref=source,
            dst_ref=target,
            send_sem=self.send_sems.at[index],
            recv_sem=self.recv_sems.at[index],
            device_id=device,
            device_id_type=pl.DeviceIdType.MESH,
        )
        copy.start()
        self.made.append(copy)
        return copy


def kernel(
    a_hbm, c_hbm, pos_ref, loss_ref, agrad_ref, cgrad_ref,
    a_ref, c_ref, c_hi, c_lo, ct_hi, ct_lo, al_hi, al_lo, as_hi, as_lo,
    p_ref, w_hi, w_lo, stat, back, stat_rx, loss_rx,
    blocks, pair_rx, q0, q1, qa, qb, qo, rx0, ry1, from_y, from_x, grad, far_rx, z_rx,
    in_sems, send_sems, recv_sems,
):
    anc = lax.axis_index("anc")
    z = lax.axis_index("cand")
    x, y, core = anc // 8, lax.rem(anc // 2, 4), lax.rem(anc, 2)

    def at(dx=0, dy=0, other=False, dz=0):
        px = lax.rem(x + dx, 4)
        py = lax.rem(y + dy, 4)
        pc = 1 - core if other else core
        return ((px * 4 + py) * 2 + pc, lax.rem(z + dz, 8))

    peers = [at(other=True)]
    peers += [at(dx=d) for d in (1, 2, 3)] + [at(dy=d) for d in (1, 2, 3)]
    peers += [at(dz=d) for d in range(1, 8)]
    barrier = pltpu.get_barrier_semaphore()
    for peer in peers:
        pl.semaphore_signal(barrier, inc=1, device_id=peer, device_id_type=pl.DeviceIdType.MESH)

    copies = Copies(send_sems, recv_sems)
    iota = lax.broadcasted_iota(jnp.int32, (TILE, 1), 0)

    def load_tile(j):
        rows = pl.ds(pl.multiple_of(j * TILE, TILE), TILE)
        return pltpu.make_async_copy(c_hbm.at[rows], c_ref.at[rows], in_sems.at[j])

    a_copy = pltpu.make_async_copy(a_hbm, a_ref, in_sems.at[TILES])
    a_copy.start()
    for j in range(TILES):
        load_tile(j).start()
    a_copy.wait()
    al_hi[...], al_lo[...] = split(a_ref[...] * (SCALE * LOG2E))
    as_hi[...], as_lo[...] = split(a_ref[...] * SCALE)

    def logits_half(half):
        @pl.loop(0, TILES // 2)
        def _(step):
            for sub in range(2):
                j = step * 2 + sub
                rows = pl.ds(pl.multiple_of(j * TILE, TILE), TILE)
                if half == 0:
                    load_tile(j).wait()
                    block = c_ref[rows, :]
                    ch, cl = split(block)
                    c_hi[rows, :], c_lo[rows, :] = ch, cl
                    th, tl = split((block * SCALE).T)
                    ct_hi[j], ct_lo[j] = th, tl
                else:
                    ch, cl = c_hi[rows, :], c_lo[rows, :]
                left = jnp.concatenate([ch, cl, ch], axis=1)
                first = z * CANDS + j * TILE
                for i in (2 * half, 2 * half + 1):
                    lanes = slice(i * 256, (i + 1) * 256)
                    ah, al = al_hi[lanes, :], al_lo[lanes, :]
                    logits = dot_nt(left, jnp.concatenate([ah, ah, al], axis=1))
                    place = jnp.concatenate([pos_ref[2 * i], pos_ref[2 * i + 1]], axis=1)
                    hit = iota == place - first
                    top = jnp.max(logits, axis=0, keepdims=True)
                    stat[j, 2:3, lanes] = jnp.sum(jnp.where(hit, logits, 0.0), axis=0, keepdims=True)
                    prob = jnp.exp2(logits - top)
                    stat[j, 0:1, lanes] = top
                    stat[j, 1:2, lanes] = jnp.sum(prob, axis=0, keepdims=True)
                    p_ref[2 * i, rows, :] = prob[:, :128]
                    p_ref[2 * i + 1, rows, :] = prob[:, 128:]

    def send_stats(half):
        lanes = slice(half * 512, (half + 1) * 512)
        tops = [stat[j, 0:1, lanes] for j in range(TILES)]
        top = tops[0]
        for j in range(1, TILES):
            top = jnp.maximum(top, tops[j])
        total = jnp.zeros_like(top)
        chosen = jnp.zeros_like(top)
        for j in range(TILES):
            total += stat[j, 1:2, lanes] * jnp.exp2(tops[j] - top)
            chosen += stat[j, 2:3, lanes]
        for k in range(4):
            part = slice(k * 128, (k + 1) * 128)
            stat_rx[half, z, 0, k:k + 1, :] = top[:, part]
            stat_rx[half, z, 1, k:k + 1, :] = total[:, part]
            stat_rx[half, z, 2, k:k + 1, :] = chosen[:, part]
        mine = stat_rx.at[half, z]
        return [copies.start(mine, mine, at(dz=d)) for d in (4, 3, 5, 2, 6, 1, 7)]

    def take_stats(half, sent):
        for copy in sent:
            copy.wait_recv()
        top = stat_rx[half, 0, 0, 0:4, :]
        for k in range(1, 8):
            top = jnp.maximum(top, stat_rx[half, k, 0, 0:4, :])
        total = jnp.zeros_like(top)
        chosen = jnp.zeros_like(top)
        for k in range(8):
            total += stat_rx[half, k, 1, 0:4, :] * jnp.exp2(stat_rx[half, k, 0, 0:4, :] - top)
            chosen += stat_rx[half, k, 2, 0:4, :]
        lse = top + jnp.log2(total)
        loss_rx[0, core, half * 4:half * 4 + 4, :] = (lse - chosen) * LN2
        for k in range(4):
            chunk = half * 4 + k
            for j in range(TILES):
                back[chunk, j] = jnp.exp2(stat[j, 0:1, chunk * 128:(chunk + 1) * 128] - lse[k:k + 1, :])

    def cand_part(start, count, half):
        rows = pl.ds(pl.multiple_of(start, count), count)
        first = z * CANDS + start
        j = start // TILE
        highs, lows = [], []
        for k in range(4 * half, 4 * half + 4):
            weight = p_ref[k, rows, :] * back[k, j]
            hit = iota[:count] == pos_ref[k] - first
            wh, wl = split(jnp.where(hit, weight - 1.0, weight))
            w_hi[k, rows, :], w_lo[k, rows, :] = wh, wl
            highs.append(wh)
            lows.append(wl)
        wh, wl = jnp.concatenate(highs, axis=1), jnp.concatenate(lows, axis=1)
        ah = as_hi[half * 512:(half + 1) * 512, :]
        al = as_lo[half * 512:(half + 1) * 512, :]
        return dot(wh, ah) + dot(wl, ah) + dot(wh, al)

    def cand_first():
        @pl.loop(0, TILES // 2)
        def _(step):
            for sub in range(2):
                start = (step * 2 + sub) * TILE
                c_ref[pl.ds(pl.multiple_of(start, TILE), TILE), :] = cand_part(start, TILE, 0)

    def cand_blocks(spot, offsets):
        for n, (dx, dy) in enumerate(offsets):
            start = (lax.rem(x + dx, 4) * 4 + lax.rem(y + dy, 4)) * BLOCK
            rows = pl.ds(pl.multiple_of(start, BLOCK), BLOCK)
            part = c_ref[rows, :] + cand_part(start, BLOCK, 1)
            blocks[spot + n, 0] = part[:128, :]
            blocks[spot + n, 1] = part[128:, :]
        held = slice(spot, spot + len(offsets))
        return copies.start(blocks.at[held, 1 - core], pair_rx.at[held], at(other=True))

    def anchor_pair(pair):
        places = [lax.rem(z + d, 8) for d in pair]
        acc = None
        for j in range(TILES):
            rows = slice(j * TILE, (j + 1) * TILE)
            wh = jnp.concatenate([w_hi[p, rows, :] for p in places], axis=1)
            wl = jnp.concatenate([w_lo[p, rows, :] for p in places], axis=1)
            part = dot(ct_hi[j], wh) + dot(ct_lo[j], wh) + dot(ct_hi[j], wl)
            acc = part if acc is None else acc + part
        for n, d in enumerate(pair):
            grad[d] = acc[:, n * 128:(n + 1) * 128]

    logits_half(0)
    pl.semaphore_wait(barrier, len(peers))
    stats0 = send_stats(0)
    logits_half(1)
    stats1 = send_stats(1)
    take_stats(0, stats0)
    cand_first()
    take_stats(1, stats1)
    loss_copies = [copies.start(loss_rx.at[0, core], loss_rx.at[0, core], at(other=True))]

    pairs = [cand_blocks(3 * i, [(dx, dy) for dy in AWAY]) for i, dx in enumerate(AWAY)]
    pairs.append(cand_blocks(9, [(0, dy) for dy in AWAY]))
    pairs.append(cand_blocks(12, [(dx, 0) for dx in AWAY]))
    pairs.append(cand_blocks(15, [(0, 0)]))

    def paired(spot):
        return blocks[spot, core] + pair_rx[spot]

    def far_sum(i):
        pairs[i].wait_recv()
        for k in range(3):
            both = paired(3 * i + k)
            q0[i, k] = both[:, :128]
            q1[k, i] = both[:, 128:]

    top, low = slice(0, 64), slice(64, 128)

    def ring_far(ring, land, right, left):
        return [
            copies.start(ring.at[0, :, top], land.at[0], right),
            copies.start(ring.at[0, :, low], land.at[2], left),
        ]

    def ring_plain(ring, land, right, left):
        return [
            copies.start(ring.at[1, :, low], land.at[4], right),
            copies.start(ring.at[2, :, top], land.at[5], left),
        ]

    def ring_relay(ring, land, right, left, far):
        far[0].wait_recv()
        ring[1, :, top] = ring[1, :, top] + land[0]
        near = [copies.start(ring.at[1, :, top], land.at[1], right)]
        far[1].wait_recv()
        ring[2, :, low] = ring[2, :, low] + land[2]
        near.append(copies.start(ring.at[2, :, low], land.at[3], left))
        return near

    right_x, left_x, right_y, left_y = at(dx=1), at(dx=3), at(dy=1), at(dy=3)

    far_sum(0)
    x_far = ring_far(q0, rx0, right_x, left_x)
    for copy in loss_copies:
        copy.wait_recv()
    loss_rx[1, x] = loss_rx[0, 0] + loss_rx[0, 1]
    loss_copies = [copies.start(loss_rx.at[1, x], loss_rx.at[1, x], at(dx=d)) for d in AWAY]

    anchor_pair((4, 3))
    z_four = [
        copies.start(grad.at[4, 0:128], far_rx.at[0, 0:128], at(dz=2)),
        copies.start(grad.at[4, 128:256], far_rx.at[1, 128:256], at(dz=6)),
    ]
    z_three = [copies.start(grad.at[3], far_rx.at[2], at(dz=1))]
    far_sum(1)
    far_sum(2)
    y_far = ring_far(q1, ry1, right_y, left_y)
    x_near = ring_plain(q0, rx0, right_x, left_x)
    y_near = ring_plain(q1, ry1, right_y, left_y)

    anchor_pair((5, 2))
    z_three.append(copies.start(grad.at[5], far_rx.at[3], at(dz=7)))
    x_near += ring_relay(q0, rx0, right_x, left_x, x_far)
    for i in range(3):
        pairs[3 + min(i, 2)].wait_recv()
    for k in range(3):
        qa[k] = paired(9 + k)
        qb[k] = paired(12 + k)
    qo[...] = paired(15)
    for copy in loss_copies:
        copy.wait_recv()
    loss_rx[2, y] = (loss_rx[1, 0] + loss_rx[1, 1]) + (loss_rx[1, 2] + loss_rx[1, 3])
    loss_copies = [copies.start(loss_rx.at[2, y], loss_rx.at[2, y], at(dy=d)) for d in AWAY]

    anchor_pair((6, 1))
    z_last = [copies.start(grad.at[1], z_rx.at[0], at(dz=1))]
    y_near += ring_relay(q1, ry1, right_y, left_y, y_far)
    z_four[0].wait_recv()
    z_three[0].wait_recv()
    grad[2, 0:128] = grad[2, 0:128] + far_rx[0, 0:128] + far_rx[2, 0:128]
    grad[2, 128:256] = grad[2, 128:256] + far_rx[2, 128:256]
    z_last.append(copies.start(grad.at[2], z_rx.at[1], at(dz=2)))

    anchor_pair((7, 0))
    z_last.append(copies.start(grad.at[7], z_rx.at[2], at(dz=7)))
    z_four[1].wait_recv()
    z_three[1].wait_recv()
    grad[6, 0:128] = grad[6, 0:128] + far_rx[3, 0:128]
    grad[6, 128:256] = grad[6, 128:256] + far_rx[1, 128:256] + far_rx[3, 128:256]
    z_last.append(copies.start(grad.at[6], z_rx.at[3], at(dz=6)))

    last = []
    for copy in x_near:
        copy.wait_recv()
    for k, d in enumerate(AWAY):
        qa[k, top, 0:128] = qa[k, top, 0:128] + rx0[1, k] + rx0[5, k]
        qa[k, low, 0:128] = qa[k, low, 0:128] + rx0[3, k] + rx0[4, k]
        last.append(copies.start(qa.at[k], from_y.at[k], at(dy=d)))
    for copy in y_near:
        copy.wait_recv()
    for k, d in enumerate(AWAY):
        qb[k, top, 128:256] = qb[k, top, 128:256] + ry1[1, k] + ry1[5, k]
        qb[k, low, 128:256] = qb[k, low, 128:256] + ry1[3, k] + ry1[4, k]
        last.append(copies.start(qb.at[k], from_x.at[k], at(dx=d)))

    for copy in loss_copies:
        copy.wait_recv()
    losses = (loss_rx[2, 0] + loss_rx[2, 1]) + (loss_rx[2, 2] + loss_rx[2, 3])
    loss_ref[...] = jnp.sum(losses, keepdims=True) * (1.0 / (32 * ANCHORS))
    for copy in z_last:
        copy.wait_recv()
    agrad_ref[...] = (grad[0] + (z_rx[0] + z_rx[1]) + (z_rx[2] + z_rx[3])).T
    for copy in last:
        copy.wait_recv()
    cgrad_ref[...] = (
        qo[...] + (from_y[0] + from_y[1] + from_y[2]) + (from_x[0] + from_x[1] + from_x[2])
    )
    for copy in copies.made:
        copy.wait_send()


def body(anchors, candidates, positives):
    vmem = pl.BlockSpec(memory_space=pltpu.VMEM)
    hbm = pl.BlockSpec(memory_space=pl.ANY)
    sems = 64
    loss, anchor_grad, cand_grad = pl.pallas_call(
        kernel,
        out_shape=[
            jax.ShapeDtypeStruct((1, 1), F32),
            jax.ShapeDtypeStruct((128, WIDTH), F32),
            jax.ShapeDtypeStruct((128, WIDTH), F32),
        ],
        in_specs=[hbm, hbm, vmem],
        out_specs=[vmem] * 3,
        scratch_shapes=[
            pltpu.VMEM((ANCHORS, WIDTH), F32),
            pltpu.VMEM((CANDS, WIDTH), F32),
            pltpu.VMEM((CANDS, WIDTH), BF16),
            pltpu.VMEM((CANDS, WIDTH), BF16),
            pltpu.VMEM((TILES, WIDTH, TILE), BF16),
            pltpu.VMEM((TILES, WIDTH, TILE), BF16),
            pltpu.VMEM((ANCHORS, WIDTH), BF16),
            pltpu.VMEM((ANCHORS, WIDTH), BF16),
            pltpu.VMEM((ANCHORS, WIDTH), BF16),
            pltpu.VMEM((ANCHORS, WIDTH), BF16),
            pltpu.VMEM((8, CANDS, 128), F32),
            pltpu.VMEM((8, CANDS, 128), BF16),
            pltpu.VMEM((8, CANDS, 128), BF16),
            pltpu.VMEM((TILES, 8, ANCHORS), F32),
            pltpu.VMEM((8, TILES, 1, 128), F32),
            pltpu.VMEM((2, 8, 3, 8, 128), F32),
            pltpu.VMEM((3, 4, 8, 128), F32),
            pltpu.VMEM((16, 2, 128, WIDTH), F32),
            pltpu.VMEM((16, 128, WIDTH), F32),
            pltpu.VMEM((3, 3, 128, 128), F32),
            pltpu.VMEM((3, 3, 128, 128), F32),
            pltpu.VMEM((3, 128, WIDTH), F32),
            pltpu.VMEM((3, 128, WIDTH), F32),
            pltpu.VMEM((128, WIDTH), F32),
            pltpu.VMEM((6, 3, 64, 128), F32),
            pltpu.VMEM((6, 3, 64, 128), F32),
            pltpu.VMEM((3, 128, WIDTH), F32),
            pltpu.VMEM((3, 128, WIDTH), F32),
            pltpu.VMEM((8, WIDTH, 128), F32),
            pltpu.VMEM((4, WIDTH, 128), F32),
            pltpu.VMEM((4, WIDTH, 128), F32),
            pltpu.SemaphoreType.DMA((TILES + 1,)),
            pltpu.SemaphoreType.DMA((sems,)),
            pltpu.SemaphoreType.DMA((sems,)),
        ],
        compiler_params=pltpu.CompilerParams(
            collective_id=0, has_side_effects=True, vmem_limit_bytes=63 << 20
        ),
    )(anchors, candidates, positives.reshape(8, 1, 128))
    return (loss.reshape(()), anchor_grad, cand_grad[None])


def solution(mesh):
    in_specs = (P("anc", None), P("cand", None), P("anc"))
    out_specs = (P(), P(("anc", "cand"), None), P("cand", "anc", None))
    return jax.shard_map(body, mesh=mesh, in_specs=in_specs, out_specs=out_specs, check_vma=False)
```

time: 231 us -> 63.4 us (0.27)
  blocking collectives: 99 us -> 0 us
  matrix products: 72.7 us -> 0 us
  Pallas kernels: 0 us -> 57.7 us
  waiting for transfers between devices: 31.9 us -> 0 us
  between operations: 15.9 us -> 2.4 us
  other arithmetic: 9.43 us -> 0 us
    psum x2 -> x0, blocking collectives: 81.7 us -> none  [the longest x1 70.6 us: body(): loss_total = lax.psum(jnp.sum(lse - positive_logit), 'anc')]
    dot_general x3 -> x0, matrix products: 72.7 us -> none  [product(): jnp.dot(left, right, precision=lax.Precision.HIGHEST, preferred_element_t...]
    pallas_call x0 -> x1, Pallas kernels: none -> 57.7 us  [body(): pl.pallas_call(kernel, out_shape=[jax.ShapeDtypeStruct((1, 1), F32), jax....]
    reduce_scatter x2 -> x0, waiting for transfers between devices: 31.9 us -> none  [the longest x1 31.9 us: body(): lax.psum_scatter(product(weights.T, anchors) * scale, 'anc', scatter_dime...]
    pmax x1 -> x0, blocking collectives: 17.3 us -> none  [body(): row_max = lax.pmax(local_max, 'cand')]
    reduce_sum x2 -> x0, other arithmetic: 9.43 us -> none  [the longest x1 8.82 us: body(): jnp.sum(jnp.where(hit, logits, jnp.zeros_like(logits)), axis=1)]
  transfers between devices with their start and end apart: 2 -> 0, of which waited for: 1 -> 0; matrix products, arithmetic and copies ran while one was open for 14% -> 0% of each run, Pallas kernels for 0% -> 0%
where the time goes in v2:
time: 63.4 us; the launch traced here: 63.2 us
  Pallas kernels  57.7 us (91%)
  local copies, waits for them, and re-layouts  3.14 us (5%)
  between operations  2.4 us (4%)
    pallas_call x1, Pallas kernels, body(): pl.pallas_call(kernel, out_shape=[jax.ShapeDtypeStruct((1, 1), F32), jax....  57.7 us
    unnamed x2, local copies, waits for them, and re-layouts  3.14 us

profile of v2, /device:TPU:1, one launch (start us, length us, event | category | flops | bytes accessed | tf_op | source)
XLA Modules:
  0.0 63.2 jit_solution(4094925575186447998)
XLA Ops:
  0.6 57.7 %shard_map.58 = (f32[1,1]{1,0:T(1,128)}, f32[128,256]{1,0:T(8,128)}, f32[128,256]{1,0:T(8,128)}) custom-call(f32[1024,256]{1,0:T(8,128)} %a_hbm.1, f32[4096,256]{1,0:T(8,128)} %c_hbm.1, s32[8,1,128]{2,1,0:T(1,128)} %bitcast.4), custom_call_target="tpu_custom_call" | custom-call | tf_op jit(solution)/shard_map/pallas_call | solution.py:344
  59.0 1.6 %copy.10 = f32[128,256]{1,0:T(8,128)} copy(f32[128,256]{1,0:T(8,128)} %get-tuple-element.13) | data formatting | bytes 262144
  60.5 1.6 %copy.11 = f32[1,128,256]{2,1,0:T(8,128)} copy(f32[1,128,256]{2,1,0:T(8,128)} %bitcast.3) | data formatting | bytes 262144

commit v3 on v2

v3 whole, which is shorter than its diff:
```python
import math

import jax
import jax.numpy as jnp
from jax import lax
from jax.experimental import pallas as pl
from jax.experimental.pallas import tpu as pltpu
from jax.sharding import PartitionSpec as P

F32 = jnp.float32
BF16 = jnp.bfloat16
WIDTH = 256
ANCHORS = 1024
CANDS = 4096
TILE = 512
TILES = CANDS // TILE
LOG2E = math.log2(math.e)
LN2 = math.log(2.0)
SCALE = 0.25 / math.sqrt(WIDTH)
BLOCK = 256
PARTS = ((0, 6), (6, 8))
AWAY = (2, 1, 3)


def split(value):
    high = value.astype(BF16)
    return high, (value - high.astype(F32)).astype(BF16)


def dot(left, right):
    return jnp.dot(left, right, preferred_element_type=F32)


def dot_nt(left, right):
    return lax.dot_general(left, right, (((1,), (1,)), ((), ())), preferred_element_type=F32)


class Copies:
    def __init__(self, send_sems, recv_sems):
        self.send_sems, self.recv_sems = send_sems, recv_sems
        self.made = []

    def start(self, source, target, device):
        index = len(self.made)
        copy = pltpu.make_async_remote_copy(
            src_ref=source,
            dst_ref=target,
            send_sem=self.send_sems.at[index],
            recv_sem=self.recv_sems.at[index],
            device_id=device,
            device_id_type=pl.DeviceIdType.MESH,
        )
        copy.start()
        self.made.append(copy)
        return copy


def kernel(
    a_hbm, c_hbm, pos_ref, loss_ref, agrad_ref, cgrad_ref,
    a_ref, c_ref, c_hi, c_lo, ct_hi, ct_lo, al_hi, al_lo, as_hi, as_lo,
    p_ref, stat, back, stat_rx, loss_rx,
    blocks, pair_rx, q0, q1, qa, qb, rx0, ry1, from_y, from_x, grad, far_rx, z_rx,
    in_sems, send_sems, recv_sems,
):
    anc = lax.axis_index("anc")
    z = lax.axis_index("cand")
    x, y, core = anc // 8, lax.rem(anc // 2, 4), lax.rem(anc, 2)

    def at(dx=0, dy=0, other=False, dz=0):
        px = lax.rem(x + dx, 4)
        py = lax.rem(y + dy, 4)
        pc = 1 - core if other else core
        return ((px * 4 + py) * 2 + pc, lax.rem(z + dz, 8))

    peers = [at(other=True)]
    peers += [at(dx=d) for d in (1, 2, 3)] + [at(dy=d) for d in (1, 2, 3)]
    peers += [at(dz=d) for d in range(1, 8)]
    barrier = pltpu.get_barrier_semaphore()
    for peer in peers:
        pl.semaphore_signal(barrier, inc=1, device_id=peer, device_id_type=pl.DeviceIdType.MESH)

    copies = Copies(send_sems, recv_sems)
    iota = lax.broadcasted_iota(jnp.int32, (TILE, 1), 0)

    def load_tile(j):
        rows = pl.ds(pl.multiple_of(j * TILE, TILE), TILE)
        return pltpu.make_async_copy(c_hbm.at[rows], c_ref.at[rows], in_sems.at[j])

    a_copy = pltpu.make_async_copy(a_hbm, a_ref, in_sems.at[TILES])
    a_copy.start()
    for j in range(TILES):
        load_tile(j).start()
    a_copy.wait()
    al_hi[...], al_lo[...] = split(a_ref[...] * (SCALE * LOG2E))
    as_hi[...], as_lo[...] = split(a_ref[...] * SCALE)

    def logits_part(part):
        tiles = range(PARTS[part][0] // 2, PARTS[part][1] // 2)
        subs = 1 if part == 0 else 4

        @pl.loop(0, TILES // subs)
        def _(step):
            for sub in range(subs):
                j = step * subs + sub
                rows = pl.ds(pl.multiple_of(j * TILE, TILE), TILE)
                if part == 0:
                    load_tile(j).wait()
                    block = c_ref[rows, :]
                    ch, cl = split(block)
                    c_hi[rows, :], c_lo[rows, :] = ch, cl
                    th, tl = split((block * SCALE).T)
                    ct_hi[j], ct_lo[j] = th, tl
                else:
                    ch, cl = c_hi[rows, :], c_lo[rows, :]
                left = jnp.concatenate([ch, cl, ch], axis=1)
                first = z * CANDS + j * TILE
                for i in tiles:
                    lanes = slice(i * 256, (i + 1) * 256)
                    ah, al = al_hi[lanes, :], al_lo[lanes, :]
                    logits = dot_nt(left, jnp.concatenate([ah, ah, al], axis=1))
                    place = jnp.concatenate([pos_ref[2 * i], pos_ref[2 * i + 1]], axis=1)
                    hit = iota == place - first
                    top = jnp.max(logits, axis=0, keepdims=True)
                    stat[j, 2:3, lanes] = jnp.sum(jnp.where(hit, logits, 0.0), axis=0, keepdims=True)
                    prob = jnp.exp2(logits - top)
                    stat[j, 0:1, lanes] = top
                    stat[j, 1:2, lanes] = jnp.sum(prob, axis=0, keepdims=True)
                    p_ref[2 * i, rows, :] = prob[:, :128]
                    p_ref[2 * i + 1, rows, :] = prob[:, 128:]

    def send_stats(part):
        lo, hi = PARTS[part]
        lanes = slice(lo * 128, hi * 128)
        tops = [stat[j, 0:1, lanes] for j in range(TILES)]
        top = tops[0]
        for j in range(1, TILES):
            top = jnp.maximum(top, tops[j])
        total = jnp.zeros_like(top)
        chosen = jnp.zeros_like(top)
        for j in range(TILES):
            total += stat[j, 1:2, lanes] * jnp.exp2(tops[j] - top)
            chosen += stat[j, 2:3, lanes]
        for k in range(hi - lo):
            piece = slice(k * 128, (k + 1) * 128)
            stat_rx[part, z, 0, k:k + 1, :] = top[:, piece]
            stat_rx[part, z, 1, k:k + 1, :] = total[:, piece]
            stat_rx[part, z, 2, k:k + 1, :] = chosen[:, piece]
        mine = stat_rx.at[part, z]
        return [copies.start(mine, mine, at(dz=d)) for d in (4, 3, 5, 2, 6, 1, 7)]

    def take_stats(part, sent):
        for copy in sent:
            copy.wait_recv()
        lo, hi = PARTS[part]
        used = slice(0, hi - lo)
        top = stat_rx[part, 0, 0, used, :]
        for k in range(1, 8):
            top = jnp.maximum(top, stat_rx[part, k, 0, used, :])
        total = jnp.zeros_like(top)
        chosen = jnp.zeros_like(top)
        for k in range(8):
            total += stat_rx[part, k, 1, used, :] * jnp.exp2(stat_rx[part, k, 0, used, :] - top)
            chosen += stat_rx[part, k, 2, used, :]
        lse = top + jnp.log2(total)
        loss_rx[0, core, lo:hi, :] = (lse - chosen) * LN2
        for k in range(lo, hi):
            for j in range(TILES):
                back[k, j] = jnp.exp2(stat[j, 0:1, k * 128:(k + 1) * 128] - lse[k - lo:k - lo + 1, :])

    def weights(k, rows, count, first, j):
        weight = p_ref[k, rows, :] * back[k, j]
        hit = iota[:count] == pos_ref[k] - first
        return split(jnp.where(hit, weight - 1.0, weight))

    def cand_blocks(spot, offsets, lo, hi):
        for n, (dx, dy) in enumerate(offsets):
            start = (lax.rem(x + dx, 4) * 4 + lax.rem(y + dy, 4)) * BLOCK
            rows = pl.ds(pl.multiple_of(start, BLOCK), BLOCK)
            both = [weights(k, rows, BLOCK, z * CANDS + start, start // TILE) for k in range(lo, hi)]
            wh = jnp.concatenate([w[0] for w in both], axis=1)
            wl = jnp.concatenate([w[1] for w in both], axis=1)
            ah, al = as_hi[lo * 128:hi * 128, :], as_lo[lo * 128:hi * 128, :]
            part = dot(wh, ah) + dot(wl, ah) + dot(wh, al)
            for c in range(2):
                mine = part[c * 128:(c + 1) * 128, :]
                blocks[spot + n, c] = mine if lo == 0 else blocks[spot + n, c] + mine

    def cand_send(spot, count):
        held = slice(spot, spot + count)
        return copies.start(blocks.at[held, 1 - core], pair_rx.at[held], at(other=True))

    def anchor_pair(pair):
        places = [lax.rem(z + d, 8) for d in pair]
        acc = None
        for j in range(TILES):
            rows = slice(j * TILE, (j + 1) * TILE)
            both = [weights(p, rows, TILE, z * CANDS + j * TILE, j) for p in places]
            wh = jnp.concatenate([w[0] for w in both], axis=1)
            wl = jnp.concatenate([w[1] for w in both], axis=1)
            part = dot(ct_hi[j], wh) + dot(ct_lo[j], wh) + dot(ct_hi[j], wl)
            acc = part if acc is None else acc + part
        for n, d in enumerate(pair):
            grad[d] = acc[:, n * 128:(n + 1) * 128]

    def paired(spot):
        return blocks[spot, core] + pair_rx[spot]

    def far_send(i):
        pairs[i].wait_recv()
        for k in range(3):
            both = paired(3 * i + k)
            q0[i, k] = both[:, :128]
            q1[i, k] = both[:, 128:]
        sent = [copies.start(q0.at[i], rx0.at[i], at(dx=AWAY[i]))]
        return sent + [copies.start(q1.at[i, k], ry1.at[i, k], at(dy=AWAY[k])) for k in range(3)]

    low, high = slice(0, 128), slice(128, 256)
    logits_part(0)
    pl.semaphore_wait(barrier, len(peers))
    stats0 = send_stats(0)
    logits_part(1)
    stats1 = send_stats(1)
    take_stats(0, stats0)
    spots = [(3 * i, [(dx, dy) for dy in AWAY]) for i, dx in enumerate(AWAY)]
    spots += [(9, [(0, dy) for dy in AWAY]), (12, [(dx, 0) for dx in AWAY])]
    for spot, offsets in spots:
        cand_blocks(spot, offsets, 0, 6)
    take_stats(1, stats1)
    loss_copies = [copies.start(loss_rx.at[0, core], loss_rx.at[0, core], at(other=True))]

    anchor_pair((4, 3))
    to_two = [
        copies.start(grad.at[4, low], far_rx.at[0, low], at(dz=2)),
        copies.start(grad.at[3], far_rx.at[2], at(dz=1)),
    ]
    to_six = [copies.start(grad.at[4, high], far_rx.at[1, high], at(dz=6))]
    pairs = []
    for spot, offsets in spots[:3]:
        cand_blocks(spot, offsets, 6, 8)
        pairs.append(cand_send(spot, 3))
    far = far_send(0) + far_send(1)

    anchor_pair((5, 2))
    to_six.append(copies.start(grad.at[5], far_rx.at[3], at(dz=7)))
    far += far_send(2)
    for copy in loss_copies:
        copy.wait_recv()
    loss_rx[1, x] = loss_rx[0, 0] + loss_rx[0, 1]
    loss_copies = [copies.start(loss_rx.at[1, x], loss_rx.at[1, x], at(dx=d)) for d in AWAY]
    for spot, offsets in spots[3:]:
        cand_blocks(spot, offsets, 6, 8)
        pairs.append(cand_send(spot, 3))

    anchor_pair((6, 1))
    z_last = [copies.start(grad.at[1], z_rx.at[0], at(dz=1))]
    last = []
    pairs[3].wait_recv()
    pairs[4].wait_recv()
    for k, d in enumerate(AWAY):
        mine = paired(9 + k)
        qa[k, 0], qa[k, 1] = mine[:, :128], mine[:, 128:]
        last.append(copies.start(qa.at[k, 1], from_y.at[k, 1], at(dy=d)))
        mine = paired(12 + k)
        qb[k, 0], qb[k, 1] = mine[:, :128], mine[:, 128:]
        last.append(copies.start(qb.at[k, 0], from_x.at[k, 0], at(dx=d)))
    for copy in loss_copies:
        copy.wait_recv()
    loss_rx[2, y] = (loss_rx[1, 0] + loss_rx[1, 1]) + (loss_rx[1, 2] + loss_rx[1, 3])
    loss_copies = [copies.start(loss_rx.at[2, y], loss_rx.at[2, y], at(dy=d)) for d in AWAY]

    anchor_pair((7, 0))
    z_last.append(copies.start(grad.at[7], z_rx.at[1], at(dz=7)))
    for copy in to_two:
        copy.wait_recv()
    grad[2, low] = grad[2, low] + far_rx[0, low] + far_rx[2, low]
    grad[2, high] = grad[2, high] + far_rx[2, high]
    z_last.append(copies.start(grad.at[2], z_rx.at[2], at(dz=2)))
    for copy in to_six:
        copy.wait_recv()
    grad[6, low] = grad[6, low] + far_rx[3, low]
    grad[6, high] = grad[6, high] + far_rx[1, high] + far_rx[3, high]
    z_last.append(copies.start(grad.at[6], z_rx.at[3], at(dz=6)))

    cand_blocks(15, [(0, 0)], 0, 8)
    pairs.append(cand_send(15, 1))
    for copy in far:
        copy.wait_recv()
    for k, d in enumerate(AWAY):
        qa[k, 0] = qa[k, 0] + (rx0[0, k] + rx0[1, k] + rx0[2, k])
        last.append(copies.start(qa.at[k, 0], from_y.at[k, 0], at(dy=d)))
        qb[k, 1] = qb[k, 1] + (ry1[k, 0] + ry1[k, 1] + ry1[k, 2])
        last.append(copies.start(qb.at[k, 1], from_x.at[k, 1], at(dx=d)))

    for copy in loss_copies:
        copy.wait_recv()
    losses = (loss_rx[2, 0] + loss_rx[2, 1]) + (loss_rx[2, 2] + loss_rx[2, 3])
    loss_ref[...] = jnp.sum(losses, keepdims=True) * (1.0 / (32 * ANCHORS))
    for copy in z_last:
        copy.wait_recv()
    agrad_ref[...] = (grad[0] + (z_rx[0] + z_rx[1]) + (z_rx[2] + z_rx[3])).T
    pairs[5].wait_recv()
    for copy in last:
        copy.wait_recv()
    own = paired(15)
    for h in range(2):
        lanes = slice(h * 128, (h + 1) * 128)
        cgrad_ref[:, lanes] = own[:, lanes] + (
            (from_y[0, h] + from_y[1, h] + from_y[2, h]) + (from_x[0, h] + from_x[1, h] + from_x[2, h])
        )
    for copy in copies.made:
        copy.wait_send()


def body(anchors, candidates, positives):
    vmem = pl.BlockSpec(memory_space=pltpu.VMEM)
    hbm = pl.BlockSpec(memory_space=pl.ANY)
    sems = 64
    grads = [jax.ShapeDtypeStruct((128, WIDTH), F32)] * 2
    loss, anchor_grad, cand_grad = pl.pallas_call(
        kernel,
        out_shape=[jax.ShapeDtypeStruct((1, 1), F32)] + grads,
        in_specs=[hbm, hbm, vmem],
        out_specs=[vmem] * 3,
        scratch_shapes=[
            pltpu.VMEM((ANCHORS, WIDTH), F32),
            pltpu.VMEM((CANDS, WIDTH), F32),
            pltpu.VMEM((CANDS, WIDTH), BF16),
            pltpu.VMEM((CANDS, WIDTH), BF16),
            pltpu.VMEM((TILES, WIDTH, TILE), BF16),
            pltpu.VMEM((TILES, WIDTH, TILE), BF16),
            pltpu.VMEM((ANCHORS, WIDTH), BF16),
            pltpu.VMEM((ANCHORS, WIDTH), BF16),
            pltpu.VMEM((ANCHORS, WIDTH), BF16),
            pltpu.VMEM((ANCHORS, WIDTH), BF16),
            pltpu.VMEM((8, CANDS, 128), F32),
            pltpu.VMEM((TILES, 8, ANCHORS), F32),
            pltpu.VMEM((8, TILES, 1, 128), F32),
            pltpu.VMEM((2, 8, 3, 8, 128), F32),
            pltpu.VMEM((3, 4, 8, 128), F32),
            pltpu.VMEM((16, 2, 128, WIDTH), F32),
            pltpu.VMEM((16, 128, WIDTH), F32),
            pltpu.VMEM((3, 3, 128, 128), F32),
            pltpu.VMEM((3, 3, 128, 128), F32),
            pltpu.VMEM((3, 2, 128, 128), F32),
            pltpu.VMEM((3, 2, 128, 128), F32),
            pltpu.VMEM((3, 3, 128, 128), F32),
            pltpu.VMEM((3, 3, 128, 128), F32),
            pltpu.VMEM((3, 2, 128, 128), F32),
            pltpu.VMEM((3, 2, 128, 128), F32),
            pltpu.VMEM((8, WIDTH, 128), F32),
            pltpu.VMEM((4, WIDTH, 128), F32),
            pltpu.VMEM((4, WIDTH, 128), F32),
            pltpu.SemaphoreType.DMA((TILES + 1,)),
            pltpu.SemaphoreType.DMA((sems,)),
            pltpu.SemaphoreType.DMA((sems,)),
        ],
        compiler_params=pltpu.CompilerParams(
            collective_id=0, has_side_effects=True, vmem_limit_bytes=63 << 20
        ),
    )(anchors, candidates, positives.reshape(8, 1, 128))
    return (loss.reshape(()), anchor_grad, cand_grad[None])


def solution(mesh):
    in_specs = (P("anc", None), P("cand", None), P("anc"))
    out_specs = (P(), P(("anc", "cand"), None), P("cand", "anc", None))
    return jax.shard_map(body, mesh=mesh, in_specs=in_specs, out_specs=out_specs, check_vma=False)
```

time: 63.4 us -> 66.8 us (1.054)
  Pallas kernels: 57.7 us -> 61.1 us
    pallas_call x1, Pallas kernels: 57.7 us -> 61.1 us  [body(): pl.pallas_call(kernel, out_shape=[jax.ShapeDtypeStruct((1, 1), F32)] + gr...]
where the time goes in v3:
time: 66.8 us; the launch traced here: 66.6 us
  Pallas kernels  61.1 us (91%)
  local copies, waits for them, and re-layouts  3.14 us (5%)
  between operations  2.4 us (4%)
    pallas_call x1, Pallas kernels, body(): pl.pallas_call(kernel, out_shape=[jax.ShapeDtypeStruct((1, 1), F32)] + gr...  61.1 us
    unnamed x2, local copies, waits for them, and re-layouts  3.14 us

profile of v3, /device:TPU:1, one launch (start us, length us, event | category | flops | bytes accessed | tf_op | source)
XLA Modules:
  0.0 66.6 jit_solution(4780855042866192580)
XLA Ops:
  0.6 61.1 %shard_map.58 = (f32[1,1]{1,0:T(1,128)}, f32[128,256]{1,0:T(8,128)}, f32[128,256]{1,0:T(8,128)}) custom-call(f32[1024,256]{1,0:T(8,128)} %a_hbm.1, f32[4096,256]{1,0:T(8,128)} %c_hbm.1, s32[8,1,128]{2,1,0:T(1,128)} %bitcast.4), custom_call_target="tpu_custom_call" | custom-call | tf_op jit(solution)/shard_map/pallas_call | solution.py:319
  62.4 1.6 %copy.10 = f32[128,256]{1,0:T(8,128)} copy(f32[128,256]{1,0:T(8,128)} %get-tuple-element.13) | data formatting | bytes 262144
  63.9 1.6 %copy.11 = f32[1,128,256]{2,1,0:T(8,128)} copy(f32[1,128,256]{2,1,0:T(8,128)} %bitcast.3) | data formatting | bytes 262144

commit v4 on v3

--- a/solution.py
+++ b/solution.py
@@ -18,7 +18,7 @@
 LN2 = math.log(2.0)
 SCALE = 0.25 / math.sqrt(WIDTH)
 BLOCK = 256
-PARTS = ((0, 6), (6, 8))
+CHUNKS = (0, 2, 4, 6, 1, 3, 5, 7)
 AWAY = (2, 1, 3)
 
 
@@ -59,7 +59,7 @@
     a_hbm, c_hbm, pos_ref, loss_ref, agrad_ref, cgrad_ref,
     a_ref, c_ref, c_hi, c_lo, ct_hi, ct_lo, al_hi, al_lo, as_hi, as_lo,
     p_ref, stat, back, stat_rx, loss_rx,
-    blocks, pair_rx, q0, q1, qa, qb, rx0, ry1, from_y, from_x, grad, far_rx, z_rx,
+    blocks, pair_rx, q0, q1, qa, qb, rx0, ry1, from_y, from_x, grad, z_rx, z_send, z_recv,
     in_sems, send_sems, recv_sems,
 ):
     anc = lax.axis_index("anc")
@@ -86,17 +86,22 @@
         rows = pl.ds(pl.multiple_of(j * TILE, TILE), TILE)
         return pltpu.make_async_copy(c_hbm.at[rows], c_ref.at[rows], in_sems.at[j])
 
-    a_copy = pltpu.make_async_copy(a_hbm, a_ref, in_sems.at[TILES])
-    a_copy.start()
+    a_copies = []
+    for q, chunk in enumerate(CHUNKS):
+        a_copies.append(pltpu.make_async_copy(
+            a_hbm.at[pl.ds(chunk * 128, 128)], a_ref.at[pl.ds(q * 128, 128)], in_sems.at[TILES + q]
+        ))
+        a_copies[-1].start()
     for j in range(TILES):
         load_tile(j).start()
-    a_copy.wait()
+    for copy in a_copies:
+        copy.wait()
     al_hi[...], al_lo[...] = split(a_ref[...] * (SCALE * LOG2E))
     as_hi[...], as_lo[...] = split(a_ref[...] * SCALE)
 
     def logits_part(part):
-        tiles = range(PARTS[part][0] // 2, PARTS[part][1] // 2)
-        subs = 1 if part == 0 else 4
+        tiles = (2 * part, 2 * part + 1)
+        subs = 2
 
         @pl.loop(0, TILES // subs)
         def _(step):
@@ -118,7 +123,7 @@
                     lanes = slice(i * 256, (i + 1) * 256)
                     ah, al = al_hi[lanes, :], al_lo[lanes, :]
                     logits = dot_nt(left, jnp.concatenate([ah, ah, al], axis=1))
-                    place = jnp.concatenate([pos_ref[2 * i], pos_ref[2 * i + 1]], axis=1)
+                    place = jnp.concatenate([pos_ref[CHUNKS[2 * i]], pos_ref[CHUNKS[2 * i + 1]]], axis=1)
                     hit = iota == place - first
                     top = jnp.max(logits, axis=0, keepdims=True)
                     stat[j, 2:3, lanes] = jnp.sum(jnp.where(hit, logits, 0.0), axis=0, keepdims=True)
@@ -129,7 +134,7 @@
                     p_ref[2 * i + 1, rows, :] = prob[:, 128:]
 
     def send_stats(part):
-        lo, hi = PARTS[part]
+        lo, hi = 4 * part, 4 * part + 4
         lanes = slice(lo * 128, hi * 128)
         tops = [stat[j, 0:1, lanes] for j in range(TILES)]
         top = tops[0]
@@ -151,7 +156,7 @@
     def take_stats(part, sent):
         for copy in sent:
             copy.wait_recv()
-        lo, hi = PARTS[part]
+        lo, hi = 4 * part, 4 * part + 4
         used = slice(0, hi - lo)
         top = stat_rx[part, 0, 0, used, :]
         for k in range(1, 8):
@@ -167,40 +172,63 @@
             for j in range(TILES):
                 back[k, j] = jnp.exp2(stat[j, 0:1, k * 128:(k + 1) * 128] - lse[k - lo:k - lo + 1, :])
 
-    def weights(k, rows, count, first, j):
-        weight = p_ref[k, rows, :] * back[k, j]
-        hit = iota[:count] == pos_ref[k] - first
+    def weights(q, chunk, rows, count, first, j):
+        weight = p_ref[q, rows, :] * back[q, j]
+        hit = iota[:count] == pos_ref[chunk] - first
         return split(jnp.where(hit, weight - 1.0, weight))
 
-    def cand_blocks(spot, offsets, lo, hi):
+    def cand_blocks(spot, offsets):
         for n, (dx, dy) in enumerate(offsets):
             start = (lax.rem(x + dx, 4) * 4 + lax.rem(y + dy, 4)) * BLOCK
             rows = pl.ds(pl.multiple_of(start, BLOCK), BLOCK)
-            both = [weights(k, rows, BLOCK, z * CANDS + start, start // TILE) for k in range(lo, hi)]
+            first = z * CANDS + start
+            both = [weights(q, CHUNKS[q], rows, BLOCK, first, start // TILE) for q in range(8)]
             wh = jnp.concatenate([w[0] for w in both], axis=1)
             wl = jnp.concatenate([w[1] for w in both], axis=1)
-            ah, al = as_hi[lo * 128:hi * 128, :], as_lo[lo * 128:hi * 128, :]
-            part = dot(wh, ah) + dot(wl, ah) + dot(wh, al)
-            for c in range(2):
-                mine = part[c * 128:(c + 1) * 128, :]
-                blocks[spot + n, c] = mine if lo == 0 else blocks[spot + n, c] + mine
+            part = dot(wh, as_hi[...]) + dot(wl, as_hi[...]) + dot(wh, as_lo[...])
+            blocks[spot + n, 0] = part[:128, :]
+            blocks[spot + n, 1] = part[128:, :]
+        return cand_send(spot, len(offsets))
 
     def cand_send(spot, count):
         held = slice(spot, spot + count)
         return copies.start(blocks.at[held, 1 - core], pair_rx.at[held], at(other=True))
 
-    def anchor_pair(pair):
-        places = [lax.rem(z + d, 8) for d in pair]
+    odd = lax.rem(z, 2)
+
+    def offset(part, k):
+        return (odd if part == 0 else 1 - odd) + 2 * k
+
+    def anchor_pair(part, pair):
+        places = [lax.rem(z + offset(part, k), 8) for k in pair]
         acc = None
         for j in range(TILES):
             rows = slice(j * TILE, (j + 1) * TILE)
-            both = [weights(p, rows, TILE, z * CANDS + j * TILE, j) for p in places]
+            both = [
+                weights(4 * part + p // 2, p, rows, TILE, z * CANDS + j * TILE, j) for p in places
+            ]
             wh = jnp.concatenate([w[0] for w in both], axis=1)
             wl = jnp.concatenate([w[1] for w in both], axis=1)
-            part = dot(ct_hi[j], wh) + dot(ct_lo[j], wh) + dot(ct_hi[j], wl)
-            acc = part if acc is None else acc + part
-        for n, d in enumerate(pair):
-            grad[d] = acc[:, n * 128:(n + 1) * 128]
+            product = dot(ct_hi[j], wh) + dot(ct_lo[j], wh) + dot(ct_hi[j], wl)
+            acc = product if acc is None else acc + product
+        for n, k in enumerate(pair):
+            grad[4 * part + k] = acc[:, n * 128:(n + 1) * 128]
+            copy = grad_copy(part, k)
+            if k == 0:
+                pl.when(odd == 1 - part)(copy.start)
+            else:
+                copy.start()
+
+    def grad_copy(part, k):
+        away = offset(part, k)
+        return pltpu.make_async_remote_copy(
+            src_ref=grad.at[4 * part + k],
+            dst_ref=z_rx.at[away],
+            send_sem=z_send.at[4 * part + k if k else 0],
+            recv_sem=z_recv.at[away],
+            device_id=(anc, lax.rem(z + away, 8)),
+            device_id_type=pl.DeviceIdType.MESH,
+        )
 
     def paired(spot):
         return blocks[spot, core] + pair_rx[spot]
@@ -214,45 +242,29 @@
         sent = [copies.start(q0.at[i], rx0.at[i], at(dx=AWAY[i]))]
         return sent + [copies.start(q1.at[i, k], ry1.at[i, k], at(dy=AWAY[k])) for k in range(3)]
 
-    low, high = slice(0, 128), slice(128, 256)
     logits_part(0)
     pl.semaphore_wait(barrier, len(peers))
     stats0 = send_stats(0)
     logits_part(1)
     stats1 = send_stats(1)
     take_stats(0, stats0)
-    spots = [(3 * i, [(dx, dy) for dy in AWAY]) for i, dx in enumerate(AWAY)]
-    spots += [(9, [(0, dy) for dy in AWAY]), (12, [(dx, 0) for dx in AWAY])]
-    for spot, offsets in spots:
-        cand_blocks(spot, offsets, 0, 6)
+    anchor_pair(0, (2, 1))
+    anchor_pair(0, (3, 0))
     take_stats(1, stats1)
     loss_copies = [copies.start(loss_rx.at[0, core], loss_rx.at[0, core], at(other=True))]
-
-    anchor_pair((4, 3))
-    to_two = [
-        copies.start(grad.at[4, low], far_rx.at[0, low], at(dz=2)),
-        copies.start(grad.at[3], far_rx.at[2], at(dz=1)),
-    ]
-    to_six = [copies.start(grad.at[4, high], far_rx.at[1, high], at(dz=6))]
-    pairs = []
-    for spot, offsets in spots[:3]:
-        cand_blocks(spot, offsets, 6, 8)
-        pairs.append(cand_send(spot, 3))
+    pairs = [cand_blocks(3 * i, [(dx, dy) for dy in AWAY]) for i, dx in enumerate(AWAY)]
     far = far_send(0) + far_send(1)
 
-    anchor_pair((5, 2))
-    to_six.append(copies.start(grad.at[5], far_rx.at[3], at(dz=7)))
+    anchor_pair(1, (2, 1))
     far += far_send(2)
     for copy in loss_copies:
         copy.wait_recv()
     loss_rx[1, x] = loss_rx[0, 0] + loss_rx[0, 1]
     loss_copies = [copies.start(loss_rx.at[1, x], loss_rx.at[1, x], at(dx=d)) for d in AWAY]
-    for spot, offsets in spots[3:]:
-        cand_blocks(spot, offsets, 6, 8)
-        pairs.append(cand_send(spot, 3))
-
-    anchor_pair((6, 1))
-    z_last = [copies.start(grad.at[1], z_rx.at[0], at(dz=1))]
+    pairs.append(cand_blocks(9, [(0, dy) for dy in AWAY]))
+    pairs.append(cand_blocks(12, [(dx, 0) for dx in AWAY]))
+
+    anchor_pair(1, (3, 0))
     last = []
     pairs[3].wait_recv()
     pairs[4].wait_recv()
@@ -268,21 +280,7 @@
     loss_rx[2, y] = (loss_rx[1, 0] + loss_rx[1, 1]) + (loss_rx[1, 2] + loss_rx[1, 3])
     loss_copies = [copies.start(loss_rx.at[2, y], loss_rx.at[2, y], at(dy=d)) for d in AWAY]
 
-    anchor_pair((7, 0))
-    z_last.append(copies.start(grad.at[7], z_rx.at[1], at(dz=7)))
-    for copy in to_two:
-        copy.wait_recv()
-    grad[2, low] = grad[2, low] + far_rx[0, low] + far_rx[2, low]
-    grad[2, high] = grad[2, high] + far_rx[2, high]
-    z_last.append(copies.start(grad.at[2], z_rx.at[2], at(dz=2)))
-    for copy in to_six:
-        copy.wait_recv()
-    grad[6, low] = grad[6, low] + far_rx[3, low]
-    grad[6, high] = grad[6, high] + far_rx[1, high] + far_rx[3, high]
-    z_last.append(copies.start(grad.at[6], z_rx.at[3], at(dz=6)))
-
-    cand_blocks(15, [(0, 0)], 0, 8)
-    pairs.append(cand_send(15, 1))
+    pairs.append(cand_blocks(15, [(0, 0)]))
     for copy in far:
         copy.wait_recv()
     for k, d in enumerate(AWAY):
@@ -295,9 +293,17 @@
         copy.wait_recv()
     losses = (loss_rx[2, 0] + loss_rx[2, 1]) + (loss_rx[2, 2] + loss_rx[2, 3])
     loss_ref[...] = jnp.sum(losses, keepdims=True) * (1.0 / (32 * ANCHORS))
-    for copy in z_last:
-        copy.wait_recv()
-    agrad_ref[...] = (grad[0] + (z_rx[0] + z_rx[1]) + (z_rx[2] + z_rx[3])).T
+    for away in range(1, 8):
+        pltpu.make_async_remote_copy(
+            src_ref=grad.at[away],
+            dst_ref=z_rx.at[away],
+            send_sem=z_send.at[away],
+            recv_sem=z_recv.at[away],
+            device_id=at(dz=1),
+            device_id_type=pl.DeviceIdType.MESH,
+        ).wait_recv()
+    near = (z_rx[1] + z_rx[2]) + (z_rx[6] + z_rx[7])
+    agrad_ref[...] = (grad[4 * odd] + near + (z_rx[3] + z_rx[4]) + z_rx[5]).T
     pairs[5].wait_recv()
     for copy in last:
         copy.wait_recv()
@@ -309,6 +315,8 @@
         )
     for copy in copies.made:
         copy.wait_send()
+    for part, k in ((0, 0), (0, 1), (0, 2), (0, 3), (1, 1), (1, 2), (1, 3)):
+        grad_copy(part, k).wait_send()
 
 
 def body(anchors, candidates, positives):
@@ -348,9 +356,10 @@
             pltpu.VMEM((3, 2, 128, 128), F32),
             pltpu.VMEM((3, 2, 128, 128), F32),
             pltpu.VMEM((8, WIDTH, 128), F32),
-            pltpu.VMEM((4, WIDTH, 128), F32),
-            pltpu.VMEM((4, WIDTH, 128), F32),
-            pltpu.SemaphoreType.DMA((TILES + 1,)),
+            pltpu.VMEM((8, WIDTH, 128), F32),
+            pltpu.SemaphoreType.DMA((8,)),
+            pltpu.SemaphoreType.DMA((8,)),
+            pltpu.SemaphoreType.DMA((TILES + 8,)),
             pltpu.SemaphoreType.DMA((sems,)),
             pltpu.SemaphoreType.DMA((sems,)),
         ],

time: 66.8 us -> 60.8 us (0.910)
  Pallas kernels: 61.1 us -> 55.1 us
    pallas_call x1, Pallas kernels: 61.1 us -> 55.1 us  [body(): pl.pallas_call(kernel, out_shape=[jax.ShapeDtypeStruct((1, 1), F32)] + gr...]
where the time goes in v4:
time: 60.8 us; the launch traced here: 60.6 us
  Pallas kernels  55.1 us (91%)
  local copies, waits for them, and re-layouts  3.14 us (5%)
  between operations  2.4 us (4%)
    pallas_call x1, Pallas kernels, body(): pl.pallas_call(kernel, out_shape=[jax.ShapeDtypeStruct((1, 1), F32)] + gr...  55.1 us
    unnamed x2, local copies, waits for them, and re-layouts  3.14 us

profile of v4, /device:TPU:1, one launch (start us, length us, event | category | flops | bytes accessed | tf_op | source)
XLA Modules:
  0.0 60.6 jit_solution(9649625391322755114)
XLA Ops:
  0.6 55.1 %shard_map.58 = (f32[1,1]{1,0:T(1,128)}, f32[128,256]{1,0:T(8,128)}, f32[128,256]{1,0:T(8,128)}) custom-call(f32[1024,256]{1,0:T(8,128)} %a_hbm.1, f32[4096,256]{1,0:T(8,128)} %c_hbm.1, s32[8,1,128]{2,1,0:T(1,128)} %bitcast.4), custom_call_target="tpu_custom_call" | custom-call | tf_op jit(solution)/shard_map/pallas_call | solution.py:327
  56.3 1.6 %copy.10 = f32[128,256]{1,0:T(8,128)} copy(f32[128,256]{1,0:T(8,128)} %get-tuple-element.13) | data formatting | bytes 262144
  57.9 1.6 %copy.11 = f32[1,128,256]{2,1,0:T(8,128)} copy(f32[1,128,256]{2,1,0:T(8,128)} %bitcast.3) | data formatting | bytes 262144

commit v5 on v4

--- a/solution.py
+++ b/solution.py
@@ -75,10 +75,6 @@
     peers = [at(other=True)]
     peers += [at(dx=d) for d in (1, 2, 3)] + [at(dy=d) for d in (1, 2, 3)]
     peers += [at(dz=d) for d in range(1, 8)]
-    barrier = pltpu.get_barrier_semaphore()
-    for peer in peers:
-        pl.semaphore_signal(barrier, inc=1, device_id=peer, device_id_type=pl.DeviceIdType.MESH)
-
     copies = Copies(send_sems, recv_sems)
     iota = lax.broadcasted_iota(jnp.int32, (TILE, 1), 0)
 
@@ -92,46 +88,49 @@
             a_hbm.at[pl.ds(chunk * 128, 128)], a_ref.at[pl.ds(q * 128, 128)], in_sems.at[TILES + q]
         ))
         a_copies[-1].start()
-    for j in range(TILES):
+        if q == 3:
+            load_tile(0).start()
+    for j in range(1, TILES):
         load_tile(j).start()
-    for copy in a_copies:
-        copy.wait()
-    al_hi[...], al_lo[...] = split(a_ref[...] * (SCALE * LOG2E))
-    as_hi[...], as_lo[...] = split(a_ref[...] * SCALE)
+    barrier = pltpu.get_barrier_semaphore()
+    for peer in peers:
+        pl.semaphore_signal(barrier, inc=1, device_id=peer, device_id_type=pl.DeviceIdType.MESH)
 
     def logits_part(part):
         tiles = (2 * part, 2 * part + 1)
-        subs = 2
-
-        @pl.loop(0, TILES // subs)
-        def _(step):
-            for sub in range(subs):
-                j = step * subs + sub
-                rows = pl.ds(pl.multiple_of(j * TILE, TILE), TILE)
-                if part == 0:
-                    load_tile(j).wait()
-                    block = c_ref[rows, :]
-                    ch, cl = split(block)
-                    c_hi[rows, :], c_lo[rows, :] = ch, cl
-                    th, tl = split((block * SCALE).T)
-                    ct_hi[j], ct_lo[j] = th, tl
-                else:
-                    ch, cl = c_hi[rows, :], c_lo[rows, :]
-                left = jnp.concatenate([ch, cl, ch], axis=1)
-                first = z * CANDS + j * TILE
-                for i in tiles:
-                    lanes = slice(i * 256, (i + 1) * 256)
-                    ah, al = al_hi[lanes, :], al_lo[lanes, :]
-                    logits = dot_nt(left, jnp.concatenate([ah, ah, al], axis=1))
-                    place = jnp.concatenate([pos_ref[CHUNKS[2 * i]], pos_ref[CHUNKS[2 * i + 1]]], axis=1)
-                    hit = iota == place - first
-                    top = jnp.max(logits, axis=0, keepdims=True)
-                    stat[j, 2:3, lanes] = jnp.sum(jnp.where(hit, logits, 0.0), axis=0, keepdims=True)
-                    prob = jnp.exp2(logits - top)
-                    stat[j, 0:1, lanes] = top
-                    stat[j, 1:2, lanes] = jnp.sum(prob, axis=0, keepdims=True)
-                    p_ref[2 * i, rows, :] = prob[:, :128]
-                    p_ref[2 * i + 1, rows, :] = prob[:, 128:]
+        lanes = slice(part * 512, (part + 1) * 512)
+        for copy in a_copies[4 * part:4 * part + 4]:
+            copy.wait()
+        al_hi[lanes, :], al_lo[lanes, :] = split(a_ref[lanes, :] * (SCALE * LOG2E))
+        if part == 1:
+            as_hi[...], as_lo[...] = split(a_ref[...] * SCALE)
+
+        for j in range(TILES):
+            rows = slice(j * TILE, (j + 1) * TILE)
+            if part == 0:
+                load_tile(j).wait()
+                block = c_ref[rows, :]
+                ch, cl = split(block)
+                c_hi[rows, :], c_lo[rows, :] = ch, cl
+                th, tl = split((block * SCALE).T)
+                ct_hi[j], ct_lo[j] = th, tl
+            else:
+                ch, cl = c_hi[rows, :], c_lo[rows, :]
+            left = jnp.concatenate([ch, cl, ch], axis=1)
+            first = z * CANDS + j * TILE
+            for i in tiles:
+                lanes = slice(i * 256, (i + 1) * 256)
+                ah, al = al_hi[lanes, :], al_lo[lanes, :]
+                logits = dot_nt(left, jnp.concatenate([ah, ah, al], axis=1))
+                place = jnp.concatenate([pos_ref[CHUNKS[2 * i]], pos_ref[CHUNKS[2 * i + 1]]], axis=1)
+                hit = iota == place - first
+                top = jnp.max(logits, axis=0, keepdims=True)
+                stat[j, 2:3, lanes] = jnp.sum(jnp.where(hit, logits, 0.0), axis=0, keepdims=True)
+                prob = jnp.exp2(logits - top)
+                stat[j, 0:1, lanes] = top
+                stat[j, 1:2, lanes] = jnp.sum(prob, axis=0, keepdims=True)
+                p_ref[2 * i, rows, :] = prob[:, :128]
+                p_ref[2 * i + 1, rows, :] = prob[:, 128:]
 
     def send_stats(part):
         lo, hi = 4 * part, 4 * part + 4
@@ -252,15 +251,22 @@
     anchor_pair(0, (3, 0))
     take_stats(1, stats1)
     loss_copies = [copies.start(loss_rx.at[0, core], loss_rx.at[0, core], at(other=True))]
-    pairs = [cand_blocks(3 * i, [(dx, dy) for dy in AWAY]) for i, dx in enumerate(AWAY)]
-    far = far_send(0) + far_send(1)
+    pairs = [cand_blocks(0, [(AWAY[0], dy) for dy in AWAY])]
+    pairs.append(cand_blocks(3, [(AWAY[1], dy) for dy in AWAY]))
+    far = far_send(0)
+    for copy in loss_copies:
+        copy.wait_recv()
+    loss_rx[1, x] = loss_rx[0, 0] + loss_rx[0, 1]
+    loss_copies = [copies.start(loss_rx.at[1, x], loss_rx.at[1, x], at(dx=d)) for d in AWAY]
+    pairs.append(cand_blocks(6, [(AWAY[2], dy) for dy in AWAY]))
+    far += far_send(1)
 
     anchor_pair(1, (2, 1))
     far += far_send(2)
     for copy in loss_copies:
         copy.wait_recv()
-    loss_rx[1, x] = loss_rx[0, 0] + loss_rx[0, 1]
-    loss_copies = [copies.start(loss_rx.at[1, x], loss_rx.at[1, x], at(dx=d)) for d in AWAY]
+    loss_rx[2, y] = (loss_rx[1, 0] + loss_rx[1, 1]) + (loss_rx[1, 2] + loss_rx[1, 3])
+    loss_copies = [copies.start(loss_rx.at[2, y], loss_rx.at[2, y], at(dy=d)) for d in AWAY]
     pairs.append(cand_blocks(9, [(0, dy) for dy in AWAY]))
     pairs.append(cand_blocks(12, [(dx, 0) for dx in AWAY]))
 
@@ -275,10 +281,6 @@
         mine = paired(12 + k)
         qb[k, 0], qb[k, 1] = mine[:, :128], mine[:, 128:]
         last.append(copies.start(qb.at[k, 0], from_x.at[k, 0], at(dx=d)))
-    for copy in loss_copies:
-        copy.wait_recv()
-    loss_rx[2, y] = (loss_rx[1, 0] + loss_rx[1, 1]) + (loss_rx[1, 2] + loss_rx[1, 3])
-    loss_copies = [copies.start(loss_rx.at[2, y], loss_rx.at[2, y], at(dy=d)) for d in AWAY]
 
     pairs.append(cand_blocks(15, [(0, 0)]))
     for copy in far:

time: 60.8 us -> 62.1 us (1.021)
  Pallas kernels: 55.1 us -> 56.4 us
    pallas_call x1, Pallas kernels: 55.1 us -> 56.4 us  [body(): pl.pallas_call(kernel, out_shape=[jax.ShapeDtypeStruct((1, 1), F32)] + gr...]
where the time goes in v5:
time: 62.1 us; the launch traced here: 62 us
  Pallas kernels  56.4 us (91%)
  local copies, waits for them, and re-layouts  3.14 us (5%)
  between operations  2.4 us (4%)
    pallas_call x1, Pallas kernels, body(): pl.pallas_call(kernel, out_shape=[jax.ShapeDtypeStruct((1, 1), F32)] + gr...  56.4 us
    unnamed x2, local copies, waits for them, and re-layouts  3.14 us

profile of v5, /device:TPU:1, one launch (start us, length us, event | category | flops | bytes accessed | tf_op | source)
XLA Modules:
  0.0 62.0 jit_solution(6817307119142828081)
XLA Ops:
  0.6 56.4 %shard_map.58 = (f32[1,1]{1,0:T(1,128)}, f32[128,256]{1,0:T(8,128)}, f32[128,256]{1,0:T(8,128)}) custom-call(f32[1024,256]{1,0:T(8,128)} %a_hbm.1, f32[4096,256]{1,0:T(8,128)} %c_hbm.1, s32[8,1,128]{2,1,0:T(1,128)} %bitcast.4), custom_call_target="tpu_custom_call" | custom-call | tf_op jit(solution)/shard_map/pallas_call | solution.py:329
  57.7 1.6 %copy.10 = f32[128,256]{1,0:T(8,128)} copy(f32[128,256]{1,0:T(8,128)} %get-tuple-element.13) | data formatting | bytes 262144
  59.3 1.6 %copy.11 = f32[1,128,256]{2,1,0:T(8,128)} copy(f32[1,128,256]{2,1,0:T(8,128)} %bitcast.3) | data formatting | bytes 262144

commit v6 on v4

--- a/solution.py
+++ b/solution.py
@@ -56,7 +56,7 @@
 
 
 def kernel(
-    a_hbm, c_hbm, pos_ref, loss_ref, agrad_ref, cgrad_ref,
+    a_hbm, c_hbm, pos_ref, loss_ref, near_ref, far_ref,
     a_ref, c_ref, c_hi, c_lo, ct_hi, ct_lo, al_hi, al_lo, as_hi, as_lo,
     p_ref, stat, back, stat_rx, loss_rx,
     blocks, pair_rx, q0, q1, qa, qb, rx0, ry1, from_y, from_x, grad, z_rx, z_send, z_recv,
@@ -75,10 +75,6 @@
     peers = [at(other=True)]
     peers += [at(dx=d) for d in (1, 2, 3)] + [at(dy=d) for d in (1, 2, 3)]
     peers += [at(dz=d) for d in range(1, 8)]
-    barrier = pltpu.get_barrier_semaphore()
-    for peer in peers:
-        pl.semaphore_signal(barrier, inc=1, device_id=peer, device_id_type=pl.DeviceIdType.MESH)
-
     copies = Copies(send_sems, recv_sems)
     iota = lax.broadcasted_iota(jnp.int32, (TILE, 1), 0)
 
@@ -92,21 +88,27 @@
             a_hbm.at[pl.ds(chunk * 128, 128)], a_ref.at[pl.ds(q * 128, 128)], in_sems.at[TILES + q]
         ))
         a_copies[-1].start()
-    for j in range(TILES):
+        if q == 3:
+            load_tile(0).start()
+    for j in range(1, TILES):
         load_tile(j).start()
-    for copy in a_copies:
-        copy.wait()
-    al_hi[...], al_lo[...] = split(a_ref[...] * (SCALE * LOG2E))
-    as_hi[...], as_lo[...] = split(a_ref[...] * SCALE)
+    barrier = pltpu.get_barrier_semaphore()
+    for peer in peers:
+        pl.semaphore_signal(barrier, inc=1, device_id=peer, device_id_type=pl.DeviceIdType.MESH)
 
     def logits_part(part):
         tiles = (2 * part, 2 * part + 1)
-        subs = 2
-
-        @pl.loop(0, TILES // subs)
+        lanes = slice(part * 512, (part + 1) * 512)
+        for copy in a_copies[4 * part:4 * part + 4]:
+            copy.wait()
+        al_hi[lanes, :], al_lo[lanes, :] = split(a_ref[lanes, :] * (SCALE * LOG2E))
+        if part == 1:
+            as_hi[...], as_lo[...] = split(a_ref[...] * SCALE)
+
+        @pl.loop(0, TILES // 2)
         def _(step):
-            for sub in range(subs):
-                j = step * subs + sub
+            for sub in range(2):
+                j = step * 2 + sub
                 rows = pl.ds(pl.multiple_of(j * TILE, TILE), TILE)
                 if part == 0:
                     load_tile(j).wait()
@@ -252,15 +254,22 @@
     anchor_pair(0, (3, 0))
     take_stats(1, stats1)
     loss_copies = [copies.start(loss_rx.at[0, core], loss_rx.at[0, core], at(other=True))]
-    pairs = [cand_blocks(3 * i, [(dx, dy) for dy in AWAY]) for i, dx in enumerate(AWAY)]
-    far = far_send(0) + far_send(1)
+    pairs = [cand_blocks(0, [(AWAY[0], dy) for dy in AWAY])]
+    pairs.append(cand_blocks(3, [(AWAY[1], dy) for dy in AWAY]))
+    far = far_send(0)
+    for copy in loss_copies:
+        copy.wait_recv()
+    loss_rx[1, x] = loss_rx[0, 0] + loss_rx[0, 1]
+    loss_copies = [copies.start(loss_rx.at[1, x], loss_rx.at[1, x], at(dx=d)) for d in AWAY]
+    pairs.append(cand_blocks(6, [(AWAY[2], dy) for dy in AWAY]))
+    far += far_send(1)
 
     anchor_pair(1, (2, 1))
     far += far_send(2)
     for copy in loss_copies:
         copy.wait_recv()
-    loss_rx[1, x] = loss_rx[0, 0] + loss_rx[0, 1]
-    loss_copies = [copies.start(loss_rx.at[1, x], loss_rx.at[1, x], at(dx=d)) for d in AWAY]
+    loss_rx[2, y] = (loss_rx[1, 0] + loss_rx[1, 1]) + (loss_rx[1, 2] + loss_rx[1, 3])
+    loss_copies = [copies.start(loss_rx.at[2, y], loss_rx.at[2, y], at(dy=d)) for d in AWAY]
     pairs.append(cand_blocks(9, [(0, dy) for dy in AWAY]))
     pairs.append(cand_blocks(12, [(dx, 0) for dx in AWAY]))
 
@@ -275,10 +284,6 @@
         mine = paired(12 + k)
         qb[k, 0], qb[k, 1] = mine[:, :128], mine[:, 128:]
         last.append(copies.start(qb.at[k, 0], from_x.at[k, 0], at(dx=d)))
-    for copy in loss_copies:
-        copy.wait_recv()
-    loss_rx[2, y] = (loss_rx[1, 0] + loss_rx[1, 1]) + (loss_rx[1, 2] + loss_rx[1, 3])
-    loss_copies = [copies.start(loss_rx.at[2, y], loss_rx.at[2, y], at(dy=d)) for d in AWAY]
 
     pairs.append(cand_blocks(15, [(0, 0)]))
     for copy in far:
@@ -302,17 +307,16 @@
             device_id=at(dz=1),
             device_id_type=pl.DeviceIdType.MESH,
         ).wait_recv()
-    near = (z_rx[1] + z_rx[2]) + (z_rx[6] + z_rx[7])
-    agrad_ref[...] = (grad[4 * odd] + near + (z_rx[3] + z_rx[4]) + z_rx[5]).T
+    near_ref[0] = (grad[4 * odd] + (z_rx[1] + z_rx[2])).T
+    far_ref[0] = ((z_rx[6] + z_rx[7]) + (z_rx[3] + z_rx[4]) + z_rx[5]).T
     pairs[5].wait_recv()
     for copy in last:
         copy.wait_recv()
     own = paired(15)
     for h in range(2):
         lanes = slice(h * 128, (h + 1) * 128)
-        cgrad_ref[:, lanes] = own[:, lanes] + (
-            (from_y[0, h] + from_y[1, h] + from_y[2, h]) + (from_x[0, h] + from_x[1, h] + from_x[2, h])
-        )
+        near_ref[1, :, lanes] = own[:, lanes] + (from_y[0, h] + from_y[1, h] + from_y[2, h])
+        far_ref[1, :, lanes] = from_x[0, h] + from_x[1, h] + from_x[2, h]
     for copy in copies.made:
         copy.wait_send()
     for part, k in ((0, 0), (0, 1), (0, 2), (0, 3), (1, 1), (1, 2), (1, 3)):
@@ -323,8 +327,8 @@
     vmem = pl.BlockSpec(memory_space=pltpu.VMEM)
     hbm = pl.BlockSpec(memory_space=pl.ANY)
     sems = 64
-    grads = [jax.ShapeDtypeStruct((128, WIDTH), F32)] * 2
-    loss, anchor_grad, cand_grad = pl.pallas_call(
+    grads = [jax.ShapeDtypeStruct((2, 128, WIDTH), F32)] * 2
+    loss, near, far = pl.pallas_call(
         kernel,
         out_shape=[jax.ShapeDtypeStruct((1, 1), F32)] + grads,
         in_specs=[hbm, hbm, vmem],
@@ -367,7 +371,7 @@
             collective_id=0, has_side_effects=True, vmem_limit_bytes=63 << 20
         ),
     )(anchors, candidates, positives.reshape(8, 1, 128))
-    return (loss.reshape(()), anchor_grad, cand_grad[None])
+    return (loss.reshape(()), near[0] + far[0], near[1:] + far[1:])
 
 
 def solution(mesh):

time: 60.8 us -> 59.5 us (0.979)
  local copies, waits for them, and re-layouts: 3.14 us -> 0 us
  other arithmetic: 0 us -> 1.83 us
    unnamed x2 -> x0, local copies, waits for them, and re-layouts: 3.14 us -> none
    add x0 -> x1, other arithmetic: none -> 1.83 us  [body(): return (loss.reshape(()), near[0] + far[0], near[1:] + far[1:])]
where the time goes in v6:
time: 59.5 us; the launch traced here: 59.3 us
  Pallas kernels  55.1 us (93%)
  between operations  2.4 us (4%)
  other arithmetic  1.83 us (3%)
    pallas_call x1, Pallas kernels, body(): pl.pallas_call(kernel, out_shape=[jax.ShapeDtypeStruct((1, 1), F32)] + gr...  55.1 us
    add x1, other arithmetic, body(): return (loss.reshape(()), near[0] + far[0], near[1:] + far[1:])  1.83 us

profile of v6, /device:TPU:1, one launch (start us, length us, event | category | flops | bytes accessed | tf_op | source)
XLA Modules:
  0.0 59.3 jit_solution(1521812272356745919)
XLA Ops:
  0.6 55.1 %shard_map.58 = (f32[1,1]{1,0:T(1,128)}, f32[2,128,256]{2,1,0:T(8,128)}, f32[2,128,256]{2,1,0:T(8,128)}) custom-call(f32[1024,256]{1,0:T(8,128)} %a_hbm.1, f32[4096,256]{1,0:T(8,128)} %c_hbm.1, s32[8,1,128]{2,1,0:T(1,128)} %bitcast.4), custom_call_target="tpu_custom_call" | custom-call | tf_op jit(solution)/shard_map/pallas_call | solution.py:331
  55.7 1.8 %slice_add_fusion = (f32[1,128,256]{2,1,0:T(8,128)}, f32[128,256]{1,0:T(8,128)}) fusion(f32[2,128,256]{2,1,0:T(8,128)} %get-tuple-element.8, f32[2,128,256]{2,1,0:T(8,128)} %get-tuple-element.7), kind=kLoop, calls=%fused_computation | loop fusion | flops 65536 | bytes 786432 | tf_op jit(solution)/shard_map/add | solution.py:374
